TPU v7x, 128 devices: a whole 4x4x4 slice. The times are simulated.
128 devices in a mesh: req: 32 (over y, z, core), exp: 4 (over x).
Axes of the slice: x: 4, y: 4, z: 4, core: 2. Of those that a mesh axis runs over, the one named last changes fastest.
Arguments:
- queries: bfloat16 [64, 32, 6144], P('req', None, 'exp'), may hold values from -6 to 6
- cache_keys: bfloat16 [64, 512, 512], P('req', None, 'exp'), may hold values from -6 to 6
- cache_values: bfloat16 [64, 512, 512], P('req', None, 'exp'), may hold values from -6 to 6
- new_keys: bfloat16 [64, 32, 512], P('req', None, 'exp'), may hold values from -6 to 6
- new_values: bfloat16 [64, 32, 512], P('req', None, 'exp'), may hold values from -6 to 6
- counts: int32 [64], P('req'), may hold values from 1 to 32, as said below
- lengths: int32 [64], P('req'), may hold values from 2 to 512, as said below
- residual: bfloat16 [2048, 5120], P(('req', 'exp')), may hold values from -6 to 6
- o_weight: bfloat16 [6144, 5120], P('exp', 'req'), may hold values from -0.5 to 0.5
- norm_gain: float32 [5120], replicated, may hold values from 0.1 to 1.9
- expert_ids: int32 [2048, 8], P(('req', 'exp')), may hold values from 0 to 127, all different within a row; in each aligned block of 16 rows (0 to 15, 16 to 31, ...) at most 2 rows name the same one
- route_weights: float32 [2048, 8], P(('req', 'exp')), may hold values from 0.1 to 1
- gate_weight: bfloat16 [128, 5120, 768], P(('req', 'exp')), may hold values from -0.078125 to 0.078125
- up_weight: bfloat16 [128, 5120, 768], P(('req', 'exp')), may hold values from -0.078125 to 0.078125
- down_weight: bfloat16 [128, 768, 5120], P(('req', 'exp')), may hold values from -0.21875 to 0.21875
Outputs:
- mixed: bfloat16 [2048, 5120], P(('req', 'exp'))
Inputs may be any that keep to these rules, and one draw needn't show every extreme that they name: `counts`: some request has exactly 32 forced tokens. `lengths`: some request has exactly 512 cached positions. `expert_ids`: each token slot names 8 different experts. Among the rows of one device (aligned blocks of 16 rows), at most 2 name one expert.
All inputs are finite; a program needn't handle non-finite values.
Results may differ from a plain program's by a relative error of at most 0.0075.
Values may be sent and summed in bfloat16 or wider, within the bound.
No kernel may reach another device: no remote copies, remote signals or barrier semaphores. Data moves between devices by JAX's collectives and lax.ppermute only.
A program may use at most 128 MiB of HBM per device.

v0:
```python
import math

import jax
import jax.numpy as jnp
from jax import lax
from jax.sharding import PartitionSpec as P

HEAD_DIM = 128
TOPK = 8


def visible(slot_count, cached, counts, lengths):
    position = jnp.arange(cached + slot_count, dtype=jnp.int32)
    fresh_index = position - cached
    slot_index = jnp.arange(slot_count, dtype=jnp.int32)
    cache_ok = position[None, None, :] < lengths[:, None, None]
    newer_ok = (fresh_index[None, None, :] <= slot_index[None, :, None]) & (
        fresh_index[None, None, :] < counts[:, None, None]
    )
    return jnp.where(position[None, None, :] < cached, cache_ok, newer_ok)


def attend(queries, cache_keys, cache_values, new_keys, new_values, counts, lengths):
    requests, slot_count, head_width = queries.shape
    cached = cache_keys.shape[1]
    key_heads = cache_keys.shape[2] // HEAD_DIM
    grouped = head_width // (key_heads * HEAD_DIM)
    query_heads = queries.reshape(requests, slot_count, key_heads, grouped, HEAD_DIM)
    keys_joined = jnp.concatenate([cache_keys, new_keys], axis=1).reshape(
        requests, cached + slot_count, key_heads, HEAD_DIM
    )
    values_joined = jnp.concatenate([cache_values, new_values], axis=1).reshape(
        requests, cached + slot_count, key_heads, HEAD_DIM
    )
    scores = jnp.einsum(
        "rskgd,rpkd->rkgsp", query_heads, keys_joined, preferred_element_type=jnp.float32
    ) / math.sqrt(HEAD_DIM)
    allowed = visible(slot_count, cached, counts, lengths)
    scores = jnp.where(allowed[:, None, None], scores, -jnp.inf)
    highest = jnp.max(scores, axis=-1, keepdims=True)
    exponentials = jnp.exp(scores - highest)
    probabilities = (exponentials / jnp.sum(exponentials, axis=-1, keepdims=True)).astype(
        jnp.bfloat16
    )
    mixed_heads = jnp.einsum(
        "rkgsp,rpkd->rskgd", probabilities, values_joined, preferred_element_type=jnp.float32
    )
    return mixed_heads.reshape(requests * slot_count, head_width).astype(jnp.bfloat16)


def scale_rows(hidden_state, norm_gain):
    mean_square = jnp.mean(hidden_state * hidden_state, axis=-1, keepdims=True)
    return (hidden_state * lax.rsqrt(mean_square + 1e-05) * norm_gain).astype(jnp.bfloat16)


def expert_apply(token_rows, gate_matrix, up_matrix, down_matrix):
    gate_part = jnp.dot(token_rows, gate_matrix, preferred_element_type=jnp.float32)
    up_part = jnp.dot(token_rows, up_matrix, preferred_element_type=jnp.float32)
    inner = (jax.nn.silu(gate_part) * up_part).astype(jnp.bfloat16)
    return jnp.dot(inner, down_matrix, preferred_element_type=jnp.float32).astype(jnp.bfloat16)


def per_device(
    queries,
    cache_keys,
    cache_values,
    new_keys,
    new_values,
    counts,
    lengths,
    residual,
    o_weight,
    norm_gain,
    expert_ids,
    route_weights,
    gate_weight,
    up_weight,
    down_weight,
):
    requests, slot_count, head_width = queries.shape
    group_count = lax.axis_size("req")
    split_count = lax.axis_size("exp")
    split_index = lax.axis_index("exp")
    share_rows = requests * slot_count // split_count
    model_width = residual.shape[1]
    attended = attend(queries, cache_keys, cache_values, new_keys, new_values, counts, lengths)
    partial_sums = jnp.dot(
        lax.all_gather(attended, "req", axis=0, tiled=True),
        o_weight,
        preferred_element_type=jnp.float32,
    )
    arrived = lax.all_to_all(partial_sums, "req", split_axis=0, concat_axis=1, tiled=True)
    projected = lax.psum_scatter(arrived, "exp", scatter_dimension=0, tiled=True)
    hidden_state = residual.astype(jnp.float32) + projected
    normed = scale_rows(hidden_state, norm_gain)
    expert_total = group_count * split_count
    capacity = max(2, 2 * share_rows * TOPK // expert_total)
    pair_count = share_rows * TOPK
    destination = expert_ids.reshape(pair_count)
    onehot = (destination[:, None] == jnp.arange(expert_total, dtype=jnp.int32)[None, :]).astype(
        jnp.int32
    )
    slot_rank = jnp.sum((jnp.cumsum(onehot, axis=0) - 1) * onehot, axis=1)
    slot_key = destination * capacity + slot_rank
    matches = slot_key[None, :] == jnp.arange(expert_total * capacity, dtype=jnp.int32)[:, None]
    source_pair = jnp.sum(
        jnp.where(matches, jnp.arange(pair_count, dtype=jnp.int32)[None, :], 0), axis=1
    )
    occupied = jnp.any(matches, axis=1)
    outgoing = jnp.where(
        occupied[:, None], normed[source_pair // TOPK], jnp.zeros((), jnp.bfloat16)
    )
    outgoing = outgoing.reshape(expert_total, capacity, model_width)
    received = lax.all_to_all(outgoing, ("req", "exp"), split_axis=0, concat_axis=0, tiled=True)
    flat_rows = received.reshape(-1, received.shape[-1])
    outputs = expert_apply(flat_rows, gate_weight[0], up_weight[0], down_weight[0])
    results = outputs.reshape(received.shape)
    returned = lax.all_to_all(results, ("req", "exp"), split_axis=0, concat_axis=0, tiled=True)
    returned = returned.reshape(expert_total * capacity, model_width)
    pair_out = returned[slot_key]
    pair_weight = route_weights.reshape(pair_count)
    combined = jnp.sum(
        (pair_out.astype(jnp.float32) * pair_weight[:, None]).reshape(
            share_rows, TOPK, model_width
        ),
        axis=1,
    )
    token_index = split_index * share_rows + jnp.arange(share_rows, dtype=jnp.int32)
    request_of = token_index // slot_count
    slot_of = token_index % slot_count
    count_of = jnp.sum(
        jnp.where(
            request_of[:, None] == jnp.arange(requests, dtype=jnp.int32)[None, :],
            counts[None, :],
            0,
        ),
        axis=1,
    )
    live_rows = slot_of < count_of
    return jnp.where(live_rows[:, None], hidden_state + combined, 0.0).astype(jnp.bfloat16)


def solution(mesh):
    return jax.shard_map(
        per_device,
        mesh=mesh,
        in_specs=(
            P("req", None, "exp"),
            P("req", None, "exp"),
            P("req", None, "exp"),
            P("req", None, "exp"),
            P("req", None, "exp"),
            P("req"),
            P("req"),
            P(("req", "exp"), None),
            P("exp", "req"),
            P(),
            P(("req", "exp"), None),
            P(("req", "exp"), None),
            P(("req", "exp"), None, None),
            P(("req", "exp"), None, None),
            P(("req", "exp"), None, None),
        ),
        out_specs=P(("req", "exp"), None),
        check_vma=False,
    )
```

profile of v0, /device:TPU:1, one launch (start us, length us, event | category | flops | bytes accessed | tf_op | source)
XLA Modules:
  0.0 271.5 jit_solution(3338157253878999226)
XLA Ops:
  6.5 0.0 copy-start
  6.5 0.0 copy-start.9
  6.5 0.0 copy-start.10
  6.5 0.0 all-gather.2.cloned.1.call-start
  6.6 0.8 iota_compare_fusion.3
  7.5 1.5 fusion.36
  9.0 0.6 fusion.10
  9.6 0.0 copy-done.9
  9.6 0.0 copy-done.10
  9.6 0.6 fusion.17
  10.2 0.1 copy.35
  10.3 0.7 copy.53
  11.1 0.0 all-gather.2.cloned.1.call-update
  11.1 0.0 reduce-scatter.2.cloned.1.call-start
  11.1 53.0 %all-gather.2.cloned.1.call-done = bf16[2048,1536]{1,0:T(8,128)(2,1)} async-done(((bf16[64,1536]{1,0:T(8,128)(2,1)}), bf16[2048,1536]{1,0:T(8,128)(2,1)}) %all-gather.2.cloned.1.call-update) | async-done | bytes 6291472 | tf_op jit(solution)/shard_map/all_gather | solution.py:88
  64.2 0.0 copy-done
  64.2 4.6 %fusion.37 = f32[2048,160]{1,0:T(8,128)S(1)} fusion(bf16[2048,1536]{1,0:T(8,128)(2,1)} %all-gather.2.cloned.1.call-done, bf16[1536,160]{0,1:T(8,128)(2,1)S(1)} %copy-done), kind=kOutput, calls=%fused_computation.73 | convolution fusion | flops 1006632960 | bytes 8093696 | tf_op jit(solution)/shard_map/all_to_all | solution.py:92
  68.8 32.8 %all_to_all.29 = f32[32,64,160]{2,1,0:T(8,128)S(1)} all-to-all(f32[32,64,160]{2,1,0:T(8,128)S(1)} %bitcast.73), channel_id=1, replica_groups=mesh['req'=32,'exp'=4] {'req'}, dimensions={0} | all-to-all | bytes 2621440 | tf_op jit(solution)/shard_map/all_to_all | solution.py:92
  101.6 1.2 copy.37
  102.8 0.0 copy-start.6
  102.8 0.0 copy-start.4
  102.9 0.0 copy-start.5
  102.9 2.7 %all_to_all.23 = f32[64,5120]{1,0:T(8,128)} reshape(f32[64,32,160]{2,1,0:T(8,128)S(1)} %copy.37) | data formatting | bytes 2621440 | tf_op jit(solution)/shard_map/all_to_all | solution.py:92
  105.6 0.0 reduce-scatter.2.cloned.1.call-update
  105.6 0.0 copy-done.6
  105.6 0.1 copy.38
  105.7 0.1 reshape.293
  105.8 0.1 fusion.29
  105.9 0.2 reduce_window_sum.11
  106.1 0.2 select_reduce_fusion.1
  106.3 0.1 fusion.28
  106.4 0.2 broadcast_in_dim.108
  106.5 0.1 select_reduce_fusion
  106.7 19.8 %reduce-scatter.2.cloned.1.call-done = f32[16,5120]{1,0:T(8,128)} async-done(((f32[64,5120]{1,0:T(8,128)}), f32[16,5120]{1,0:T(8,128)}) %reduce-scatter.2.cloned.1.call-update) | async-done | bytes 327696 | tf_op jit(solution)/shard_map/reduce_scatter | solution.py:93
  126.5 0.0 copy-done.4
  126.5 1.1 multiply_reduce_fusion
  127.7 0.0 copy-done.5
  127.7 1.1 multiply_convert_fusion
  128.8 2.1 gather_fusion
  130.8 2.5 gather.9
  133.3 4.1 %broadcast_select_fusion = bf16[128,2,5120]{2,1,0:T(2,128)(2,1)S(1)} fusion(bf16[128,2,5120]{2,1,0:T(2,128)(2,1)} %gather.9, pred[128,2]{1,0:T(8,128)(4,1)S(1)} %broadcast_in_dim.108), kind=kLoop, calls=%fused_computation.9 | loop fusion | flops 1310720 | bytes 5243136 | tf_op jit(solution)/shard_map/jit(_where)/select_n | solution.py:110
  137.4 45.7 %all_to_all.30 = bf16[128,2,5120]{2,1,0:T(2,128)(2,1)S(1)} all-to-all(bf16[128,2,5120]{2,1,0:T(2,128)(2,1)S(1)} %broadcast_select_fusion), channel_id=1, replica_groups=mesh['req'=32,'exp'=4] {'req','exp'}, dimensions={0} | all-to-all | bytes 5242880 | tf_op jit(solution)/shard_map/all_to_all | solution.py:114
  183.1 2.4 reshape.294
  185.5 0.0 copy-start.3
  185.5 7.3 %fusion.4 = f32[256,768]{1,0:T(8,128)} fusion(bf16[256,5120]{1,0:T(8,128)(2,1)} %reshape.294, bf16[1,5120,768]{2,1,0:T(8,128)(2,1)} %param.27), kind=kOutput, calls=%fused_computation.6 | convolution fusion | flops 2013265920 | bytes 11272192 | tf_op jit(solution)/shard_map/dot_general | solution.py:57
  192.8 0.0 copy-done.3
  192.8 12.6 %fusion.6 = bf16[256,5120]{1,0:T(8,128)(2,1)} fusion(bf16[1,768,5120]{2,1,0:T(8,128)(2,1)} %param.29, bf16[256,5120]{1,0:T(8,128)(2,1)S(1)} %copy-done.3, bf16[1,5120,768]{2,1,0:T(8,128)(2,1)} %param.28, f32[256,768]{1,0:T(8,128)} %fusion.4), kind=kOutput, calls=%fused_computation.8 | convolution fusion | flops 4029022208 | bytes 21757952 | tf_op jit(solution)/shard_map/dot_general | solution.py:60
  205.4 6.3 %reshape.295 = bf16[128,2,5120]{2,1,0:T(2,128)(2,1)} reshape(bf16[256,5120]{1,0:T(8,128)(2,1)} %fusion.6) | data formatting | bytes 5242880 | tf_op jit(solution)/shard_map/reshape | solution.py:117
  211.7 5.0 %all-to-all-start.2 = ((bf16[128,2,5120]{2,1,0:T(2,128)(2,1)}), bf16[128,2,5120]{2,1,0:T(2,128)(2,1)}, u32[]{:S(2)}, u32[]{:S(2)}) async-start(bf16[128,2,5120]{2,1,0:T(2,128)(2,1)} %reshape.295), calls=%async_computation.3 | async-start | bytes 5242880 | tf_op jit(solution)/shard_map/all_to_all | solution.py:118
  216.7 0.1 copy.39
  216.8 0.1 mul.78
  216.9 0.0 copy-done.7
  216.9 0.1 copy.40
  217.0 0.0 copy-done.8
  217.0 0.1 fusion.30
  217.1 35.8 %all-to-all-done.2 = bf16[128,2,5120]{2,1,0:T(2,128)(2,1)} async-done(((bf16[128,2,5120]{2,1,0:T(2,128)(2,1)}), bf16[128,2,5120]{2,1,0:T(2,128)(2,1)}, u32[]{:S(2)}, u32[]{:S(2)}) %all-to-all-start.2) | async-done | bytes 2621472 | tf_op jit(solution)/shard_map/all_to_all | solution.py:118
  253.0 5.3 %reshape.296 = bf16[256,5120]{1,0:T(8,128)(2,1)S(1)} reshape(bf16[128,2,5120]{2,1,0:T(2,128)(2,1)} %all-to-all-done.2) | data formatting | bytes 5242880 | tf_op jit(solution)/shard_map/reshape | solution.py:119
  258.3 0.0 copy-start.2
  258.3 0.0 copy-start.1
  258.3 2.4 gather_fusion.1
  260.7 2.3 fusion.9
  263.0 0.0 copy-done.2
  263.0 1.7 select_convert_fusion
  264.7 0.0 copy-done.1
  (15 shorter events, 0.1 us)
Async XLA Ops:
  6.5 57.6 %copy-start = (bf16[1536,160]{0,1:T(8,128)(2,1)S(1)}, bf16[1536,160]{0,1:T(8,128)(2,1)}, u32[]{:S(2)}) copy-start(bf16[1536,160]{0,1:T(8,128)(2,1)} %param.23) | copy-start | bytes 1474564
  6.5 3.0 %copy-start.9 = (bf16[2,512,128]{2,1,0:T(8,128)(2,1)S(1)}, bf16[2,512,128]{2,1,0:T(8,128)(2,1)}, u32[]{:S(2)}) copy-start(bf16[2,512,128]{2,1,0:T(8,128)(2,1)} %param.17) | copy-start | bytes 786436
  6.5 3.0 %copy-start.10 = (bf16[2,32,128]{2,1,0:T(8,128)(2,1)S(1)}, bf16[2,32,128]{2,1,0:T(8,128)(2,1)}, u32[]{:S(2)}) copy-start(bf16[2,32,128]{2,1,0:T(8,128)(2,1)} %param.19) | copy-start | bytes 49156
  6.5 57.6 %all-gather.2.cloned.1.call-start = ((), (), s32[]{:S(2)}) async-start(), calls=%async_computation.4 | async-start | bytes 6488064 | tf_op jit(solution)/shard_map/all_gather | solution.py:88
  11.1 115.4 %reduce-scatter.2.cloned.1.call-start = ((), (), s32[]{:S(2)}) async-start(), calls=%async_computation.5 | async-start | bytes 1638400 | tf_op jit(solution)/shard_map/reduce_scatter | solution.py:93
  102.8 2.8 %copy-start.6 = (s32[16,8]{0,1:T(8,128)S(1)}, s32[16,8]{0,1:T(8,128)}, u32[]{:S(2)}) copy-start(s32[16,8]{0,1:T(8,128)} %param.25) | copy-start | bytes 1540
  102.8 23.7 %copy-start.4 = (bf16[16,5120]{1,0:T(8,128)(2,1)S(1)}, bf16[16,5120]{1,0:T(8,128)(2,1)}, u32[]{:S(2)}) copy-start(bf16[16,5120]{1,0:T(8,128)(2,1)} %param.22) | copy-start | bytes 491524
  102.9 24.8 %copy-start.5 = (f32[5120]{0:T(1024)S(1)}, f32[5120]{0:T(1024)}, u32[]{:S(2)}) copy-start(f32[5120]{0:T(1024)} %param.24) | copy-start | bytes 61444
  185.5 7.3 %copy-start.3 = (bf16[256,5120]{1,0:T(8,128)(2,1)S(1)}, bf16[256,5120]{1,0:T(8,128)(2,1)}, u32[]{:S(2)}) copy-start(bf16[256,5120]{1,0:T(8,128)(2,1)} %reshape.294) | copy-start | bytes 7864324
  211.7 5.2 %copy-start.7 = (f32[16,8]{0,1:T(8,128)S(1)}, f32[16,8]{0,1:T(8,128)}, u32[]{:S(2)}) copy-start(f32[16,8]{0,1:T(8,128)} %param.26) | copy-start | bytes 1540
  211.7 5.3 %copy-start.8 = (s32[2]{0:T(128)S(1)}, s32[2]{0:T(128)}, u32[]{:S(2)}) copy-start(s32[2]{0:T(128)} %param.20) | copy-start | bytes 28
  211.7 41.3 %all-to-all-start.2 = ((bf16[128,2,5120]{2,1,0:T(2,128)(2,1)}), bf16[128,2,5120]{2,1,0:T(2,128)(2,1)}, u32[]{:S(2)}, u32[]{:S(2)}) async-start(bf16[128,2,5120]{2,1,0:T(2,128)(2,1)} %reshape.295), calls=%async_computation.3 | async-start | bytes 5242880 | tf_op jit(solution)/shard_map/all_to_all | solution.py:118
  258.3 4.7 %copy-start.2 = (f32[16,5120]{1,0:T(8,128)S(1)}, f32[16,5120]{1,0:T(8,128)}, u32[]{:S(2)}) copy-start(f32[16,5120]{1,0:T(8,128)} %reduce-scatter.2.cloned.1.call-done) | copy-start | bytes 983044
  258.3 6.3 %copy-start.1 = (bf16[1536,160]{0,1:T(8,128)(2,1)S(1)}, bf16[1536,160]{0,1:T(8,128)(2,1)}, u32[]{:S(2)}) copy-start(bf16[1536,160]{0,1:T(8,128)(2,1)} %param.23) | copy-start | bytes 1474564
Sparse Core Ops, SparseCore 0:
  11.2 52.9 all-gather.1
  105.8 20.7 reduce-scatter.1
where the time goes:
time: 272 us
  waiting for transfers between devices  109 us (40%)
  blocking collectives  78.5 us (29%)
  matrix products  26.7 us (10%)
  local copies, waits for them, and re-layouts  26.4 us (10%)
  between operations  13.7 us (5%)
  other arithmetic  12.5 us (5%)
  starting transfers between devices  5.06 us (2%)
    all_gather x1, waiting for transfers between devices, per_device(): lax.all_gather(attended, 'req', axis=0, tiled=True)  53 us
    all_to_all x1, blocking collectives, per_device(): lax.all_to_all(outgoing, ('req', 'exp'), split_axis=0, concat_axis=0, til...  45.7 us
    all_to_all x1, waiting for transfers between devices, per_device(): lax.all_to_all(results, ('req', 'exp'), split_axis=0, concat_axis=0, tile...  35.8 us
    all_to_all x1, blocking collectives, per_device(): lax.all_to_all(partial_sums, 'req', split_axis=0, concat_axis=1, tiled=True)  32.8 us
    reduce_scatter x1, waiting for transfers between devices, per_device(): lax.psum_scatter(arrived, 'exp', scatter_dimension=0, tiled=True)  19.8 us
    dot_general x1, matrix products, expert_apply(): jnp.dot(inner, down_matrix, preferred_element_type=jnp.float32)  12.6 us
    dot_general x1, matrix products, expert_apply(): jnp.dot(token_rows, gate_matrix, preferred_element_type=jnp.float32)  7.26 us
    reshape x1, local copies, waits for them, and re-layouts, per_device(): results = outputs.reshape(received.shape)  6.29 us
  transfers between devices with their start and end apart: 3, of which 3 were waited for; matrix products, arithmetic and copies ran while one was open for 1% of the time, Pallas kernels for 0%

commit v1 on v0

v1 whole, which is shorter than its diff:
```python
import math

import jax
import jax.numpy as jnp
from jax import lax
from jax.experimental import pallas as pl
from jax.experimental.pallas import tpu as pltpu
from jax.sharding import Mesh
from jax.sharding import PartitionSpec as P

HEAD_DIM = 128
TOPK = 8
CAP = 2
LANES = 128
SEG = 8
AXES = ("y", "z", "c", "x")
BF = jnp.bfloat16
F32 = jnp.float32


def dot(a, b):
    return jnp.dot(a, b, preferred_element_type=F32)


def dot_t(a, b):
    return lax.dot_general(a, b, (((1,), (1,)), ((), ())), preferred_element_type=F32)


def vmem(n):
    return [pl.BlockSpec(memory_space=pltpu.VMEM)] * n


def attend_kernel(counts, lengths, q_ref, k_ref, v_ref, nk_ref, nv_ref, out_ref):
    requests, slots, width = q_ref.shape
    heads = width // HEAD_DIM
    cached = k_ref.shape[1]
    rows = heads * slots
    scale = 1.0 / math.sqrt(HEAD_DIM)
    slot = lax.broadcasted_iota(jnp.int32, (rows, slots), 0) % slots
    fresh = lax.broadcasted_iota(jnp.int32, (rows, slots), 1)
    position = lax.broadcasted_iota(jnp.int32, (rows, cached), 1)
    for r in range(requests):
        q = jnp.concatenate(
            [q_ref[r, :, h * HEAD_DIM : (h + 1) * HEAD_DIM] for h in range(heads)], axis=0
        )
        old = dot_t(q, k_ref[r]) * scale
        new = dot_t(q, nk_ref[r]) * scale
        old = jnp.where(position < lengths[r], old, -1e30)
        new = jnp.where((fresh <= slot) & (fresh < counts[r]), new, -1e30)
        highest = jnp.maximum(
            jnp.max(old, axis=1, keepdims=True), jnp.max(new, axis=1, keepdims=True)
        )
        old = jnp.exp(old - highest)
        new = jnp.exp(new - highest)
        total = jnp.sum(old, axis=1, keepdims=True) + jnp.sum(new, axis=1, keepdims=True)
        inverse = 1.0 / total
        mixed = dot((old * inverse).astype(BF), v_ref[r]) + dot(
            (new * inverse).astype(BF), nv_ref[r]
        )
        mixed = mixed.astype(BF)
        for h in range(heads):
            out_ref[r * slots : (r + 1) * slots, h * HEAD_DIM : (h + 1) * HEAD_DIM] = mixed[
                h * slots : (h + 1) * slots
            ]


def attend(queries, cache_keys, cache_values, new_keys, new_values, counts, lengths):
    requests, slots, width = queries.shape
    return pl.pallas_call(
        attend_kernel,
        out_shape=jax.ShapeDtypeStruct((requests * slots, width), BF),
        in_specs=[pl.BlockSpec(memory_space=pltpu.SMEM)] * 2 + vmem(5),
        out_specs=pl.BlockSpec(memory_space=pltpu.VMEM),
        compiler_params=pltpu.CompilerParams(vmem_limit_bytes=32 << 20),
        cost_estimate=pl.CostEstimate(
            flops=4 * 768 * 544 * 128, bytes_accessed=1 << 20, transcendentals=768 * 544
        ),
        name="attend",
    )(counts, lengths, queries, cache_keys, cache_values, new_keys, new_values)


def norm_kernel(arrived_ref, residual_ref, gain_ref, place_ref, hidden_ref, out_ref):
    blocks, rows, part = arrived_ref.shape
    width = residual_ref.shape[1]
    groups = width // part
    splits = blocks // groups
    square = jnp.zeros((rows, 1), F32)
    for g in range(groups):
        total = residual_ref[:, g * part : (g + 1) * part].astype(F32)
        for k in range(splits):
            total = total + arrived_ref[g * splits + k].astype(F32)
        hidden_ref[:, g * part : (g + 1) * part] = total
        square = square + jnp.sum(total * total, axis=1, keepdims=True)
    factor = lax.rsqrt(square / width + 1e-05)
    seg = width // SEG
    normed = jnp.concatenate(
        [
            (
                hidden_ref[:, s * seg : (s + 1) * seg]
                * factor
                * gain_ref[:, s * seg : (s + 1) * seg]
            ).astype(BF)
            for s in range(SEG)
        ],
        axis=0,
    )
    tile = 256
    for i in range(out_ref.shape[0] // tile):
        at = pl.ds(i * tile, tile)
        out_ref[at, :] = dot(place_ref[at, :], normed).astype(BF)


def norm_and_place(arrived, residual, gain, place):
    rows, width = residual.shape
    return pl.pallas_call(
        norm_kernel,
        out_shape=(
            jax.ShapeDtypeStruct((rows, width), F32),
            jax.ShapeDtypeStruct((place.shape[0], width // SEG), BF),
        ),
        in_specs=vmem(4),
        out_specs=tuple(vmem(2)),
        compiler_params=pltpu.CompilerParams(vmem_limit_bytes=32 << 20),
        name="norm_place",
    )(arrived, residual, gain, place)


def expert_kernel(
    x_ref, gate_hbm, up_hbm, down_hbm, out_ref, stage, gate, up, down, inner, sems
):
    rows = x_ref.shape[0] // SEG
    seg = x_ref.shape[1]
    half = gate.shape[1]
    lanes = seg // LANES

    def piece(kind, s):
        at = pl.ds(s * seg, seg)
        if kind == 0:
            return pltpu.make_async_copy(gate_hbm.at[at, :], gate.at[at, :], sems.at[0, s])
        if kind == 1:
            return pltpu.make_async_copy(up_hbm.at[at, :], up.at[at, :], sems.at[1, s])
        return pltpu.make_async_copy(down_hbm.at[:, at], down.at[:, at], sems.at[2, s])

    for s in range(SEG):
        piece(0, s).start()
        piece(1, s).start()
    for s in range(SEG):
        piece(2, s).start()
    tile = 256
    for i in range(x_ref.shape[0] // tile):
        at = pl.ds(i * tile, tile)
        for k in range(lanes):
            stage[k, at, :] = x_ref[at, k * LANES : (k + 1) * LANES].astype(F32)
    gate_sum = jnp.zeros((rows, half), F32)
    up_sum = jnp.zeros((rows, half), F32)
    for s in range(SEG):
        x = jnp.concatenate(
            [stage[k, pl.ds(s, rows, stride=SEG), :].astype(BF) for k in range(lanes)], axis=1
        )
        piece(0, s).wait()
        gate_sum = gate_sum + dot(x, gate[pl.ds(s * seg, seg), :])
        piece(1, s).wait()
        up_sum = up_sum + dot(x, up[pl.ds(s * seg, seg), :])
    inner[...] = (gate_sum / (1.0 + jnp.exp(-gate_sum)) * up_sum).astype(BF)
    for s in range(SEG):
        piece(2, s).wait()
        result = dot(inner[...], down[:, pl.ds(s * seg, seg)])
        for k in range(lanes):
            stage[k, pl.ds(s, rows, stride=SEG), :] = result[:, k * LANES : (k + 1) * LANES]
    for i in range(x_ref.shape[0] // tile):
        at = pl.ds(i * tile, tile)
        for k in range(lanes):
            out_ref[at, k * LANES : (k + 1) * LANES] = stage[k, at, :].astype(BF)


def apply_expert(rows, gate, up, down):
    count, seg = rows.shape
    width, half = gate.shape
    return pl.pallas_call(
        expert_kernel,
        out_shape=jax.ShapeDtypeStruct((count, seg), BF),
        in_specs=vmem(1) + [pl.BlockSpec(memory_space=pl.ANY)] * 3,
        out_specs=pl.BlockSpec(memory_space=pltpu.VMEM),
        scratch_shapes=[
            pltpu.VMEM((seg // LANES, count, LANES), F32),
            pltpu.VMEM((width, half), BF),
            pltpu.VMEM((width, half), BF),
            pltpu.VMEM((half, width), BF),
            pltpu.VMEM((count // SEG, half), BF),
            pltpu.SemaphoreType.DMA((3, SEG)),
        ],
        compiler_params=pltpu.CompilerParams(vmem_limit_bytes=52 << 20),
        name="expert",
    )(rows, gate, up, down)


def combine_kernel(back_ref, high_ref, low_ref, hidden_ref, live_ref, out_ref):
    rows, width = hidden_ref.shape
    seg = width // SEG
    back = back_ref[...]
    mixed = dot(high_ref[...], back) + dot(low_ref[...], back)
    live = live_ref[...] > 0
    for s in range(SEG):
        at = slice(s * seg, (s + 1) * seg)
        total = hidden_ref[:, at] + mixed[s * rows : (s + 1) * rows]
        out_ref[:, at] = jnp.where(live, total, 0.0).astype(BF)


def combine(back, high, low, hidden, live):
    return pl.pallas_call(
        combine_kernel,
        out_shape=jax.ShapeDtypeStruct(hidden.shape, BF),
        in_specs=vmem(5),
        out_specs=pl.BlockSpec(memory_space=pltpu.VMEM),
        compiler_params=pltpu.CompilerParams(vmem_limit_bytes=32 << 20),
        name="combine",
    )(back, high, low, hidden, live)


def routing(expert_ids, route_weights, experts):
    tokens = expert_ids.shape[0]
    pairs = tokens * TOPK
    destination = expert_ids.reshape(pairs)
    number = jnp.arange(pairs, dtype=jnp.int32)
    earlier = (destination[:, None] == destination[None, :]) & (number[:, None] < number[None, :])
    rank = jnp.sum(earlier.astype(jnp.int32), axis=0)
    slot = destination * CAP + rank
    match = slot[None, :] == jnp.arange(experts * CAP, dtype=jnp.int32)[:, None]
    token = jnp.sum(jnp.where(match, number[None, :] // TOPK + 1, 0), axis=1) - 1
    weight = jnp.sum(jnp.where(match, route_weights.reshape(pairs)[None, :], 0.0), axis=1)
    line = jnp.arange(experts * CAP * SEG, dtype=jnp.int32)
    token_line = jnp.repeat(token, SEG)
    key = jnp.where(token_line < 0, -1, (line % SEG) * tokens + token_line)
    weight_line = jnp.repeat(weight, SEG)
    spot = jnp.arange(SEG * tokens, dtype=jnp.int32)
    place = (key[:, None] == spot[None, :]).astype(BF)
    high = lax.reduce_precision(weight_line, 8, 7)
    low = weight_line - high
    here = spot[:, None] == key[None, :]
    return (
        place,
        jnp.where(here, high[None, :], 0.0).astype(BF),
        jnp.where(here, low[None, :], 0.0).astype(BF),
    )


def per_device(
    queries,
    cache_keys,
    cache_values,
    new_keys,
    new_values,
    counts,
    lengths,
    residual,
    o_weight,
    norm_gain,
    expert_ids,
    route_weights,
    gate_weight,
    up_weight,
    down_weight,
):
    requests, slots, _ = queries.shape
    rows, width = residual.shape
    experts = math.prod(lax.axis_size(a) for a in AXES)
    weight = lax.all_gather(o_weight.T, ("z", "c"), axis=0, tiled=True)
    attended = attend(queries, cache_keys, cache_values, new_keys, new_values, counts, lengths)
    tokens = lax.all_gather(attended, "y", axis=0, tiled=True)
    place, high, low = routing(expert_ids, route_weights, experts)
    token_index = lax.axis_index("x") * rows + jnp.arange(rows, dtype=jnp.int32)
    count_of = jnp.sum(
        jnp.where(
            (token_index // slots)[:, None] == jnp.arange(requests, dtype=jnp.int32)[None, :],
            counts[None, :],
            0,
        ),
        axis=1,
    )
    live = (token_index % slots < count_of).astype(jnp.int32)[:, None]
    partial = dot_t(tokens, weight).astype(BF)
    partial = partial.reshape(-1, rows, partial.shape[1])
    arrived = lax.all_to_all(partial, ("y", "x"), split_axis=0, concat_axis=0, tiled=True)
    hidden, outgoing = norm_and_place(arrived, residual, norm_gain[None, :], place)
    outgoing = outgoing.reshape(experts, CAP * SEG, width // SEG)
    received = lax.all_to_all(outgoing, AXES, split_axis=0, concat_axis=0, tiled=True)
    results = apply_expert(
        received.reshape(-1, width // SEG), gate_weight[0], up_weight[0], down_weight[0]
    )
    results = results.reshape(experts, CAP * SEG, width // SEG)
    back = lax.all_to_all(results, AXES, split_axis=0, concat_axis=0, tiled=True)
    return combine(back.reshape(-1, width // SEG), high, low, hidden, live)


def solution(mesh):
    fine = Mesh(mesh.devices.reshape(4, 4, 2, 4), AXES)
    req = ("y", "z", "c")
    every = AXES
    return jax.shard_map(
        per_device,
        mesh=fine,
        in_specs=(
            P(req, None, "x"),
            P(req, None, "x"),
            P(req, None, "x"),
            P(req, None, "x"),
            P(req, None, "x"),
            P(req),
            P(req),
            P(every, None),
            P("x", req),
            P(),
            P(every, None),
            P(every, None),
            P(every, None, None),
            P(every, None, None),
            P(every, None, None),
        ),
        out_specs=P(every, None),
        check_vma=False,
    )
```

time: 272 us -> 179 us (0.66)
  waiting for transfers between devices: 109 us -> 61.9 us
  Pallas kernels: 0 us -> 23.1 us
  blocking collectives: 78.5 us -> 55.4 us
  matrix products: 26.7 us -> 4.17 us
  local copies, waits for them, and re-layouts: 26.4 us -> 8.14 us
  other arithmetic: 12.5 us -> 1.79 us
  starting transfers between devices: 5.06 us -> 10.2 us
    all_gather x1, waiting for transfers between devices: 53 us -> 14.3 us  [per_device(): weight = lax.all_gather(o_weight.T, ('z', 'c'), axis=0, tiled=True)]
    all_to_all x2 -> x1, blocking collectives: 78.5 us -> 41.9 us  [per_device(): lax.all_to_all(outgoing, AXES, split_axis=0, concat_axis=0, tiled=True)]
    pallas_call x0 -> x4, Pallas kernels: none -> 23.1 us  [the longest x1 18.4 us: apply_expert(): pl.pallas_call(expert_kernel, out_shape=jax.ShapeDtypeStruct((count, seg)...]
    reduce_scatter x1 -> x0, waiting for transfers between devices: 19.8 us -> none  [per_device(): lax.psum_scatter(arrived, 'exp', scatter_dimension=0, tiled=True)]
    dot_general x4 -> x1, matrix products: 22.1 us -> 4.17 us  [dot_t(): lax.dot_general(a, b, (((1,), (1,)), ((), ())), preferred_element_type=F32)]
    reshape x4 -> x3, local copies, waits for them, and re-layouts: 14.2 us -> 0.31 us  [the longest x1 0.11 us: routing(): token_line = jnp.repeat(token, SEG)]
    all_gather x0 -> x1, blocking collectives: none -> 13.6 us  [per_device(): tokens = lax.all_gather(attended, 'y', axis=0, tiled=True)]
    all_to_all x1 -> x2, waiting for transfers between devices: 35.8 us -> 46.9 us  [the longest x1 35 us: per_device(): lax.all_to_all(results, AXES, split_axis=0, concat_axis=0, tiled=True)]
  transfers between devices with their start and end apart: 3 -> 3, of which waited for: 3 -> 3; matrix products, arithmetic and copies ran while one was open for 1% -> 2% of each run, Pallas kernels for 0% -> 1%
where the time goes in v1:
time: 179 us; the launch traced here: 178 us
  waiting for transfers between devices  61.9 us (35%)
  blocking collectives  55.4 us (31%)
  Pallas kernels  23.1 us (13%)
  between operations  13.5 us (8%)
  starting transfers between devices  10.2 us (6%)
  local copies, waits for them, and re-layouts  8.14 us (5%)
  matrix products  4.17 us (2%)
  other arithmetic  1.79 us (1%)
    all_to_all x1, blocking collectives, per_device(): lax.all_to_all(outgoing, AXES, split_axis=0, concat_axis=0, tiled=True)  41.9 us
    all_to_all x1, waiting for transfers between devices, per_device(): lax.all_to_all(results, AXES, split_axis=0, concat_axis=0, tiled=True)  35 us
    pallas_call x1, Pallas kernels, apply_expert(): pl.pallas_call(expert_kernel, out_shape=jax.ShapeDtypeStruct((count, seg)...  18.4 us
    all_gather x1, waiting for transfers between devices, per_device(): weight = lax.all_gather(o_weight.T, ('z', 'c'), axis=0, tiled=True)  14.3 us
    all_gather x1, blocking collectives, per_device(): tokens = lax.all_gather(attended, 'y', axis=0, tiled=True)  13.6 us
    all_to_all x1, waiting for transfers between devices, per_device(): lax.all_to_all(partial, ('y', 'x'), split_axis=0, concat_axis=0, tiled=True)  11.9 us
    unnamed x26, local copies, waits for them, and re-layouts  7.46 us
    all_to_all x1, starting transfers between devices, per_device(): lax.all_to_all(partial, ('y', 'x'), split_axis=0, concat_axis=0, tiled=True)  6.53 us
  transfers between devices with their start and end apart: 3, of which 3 were waited for; matrix products, arithmetic and copies ran while one was open for 2% of the time, Pallas kernels for 1%

profile of v1, /device:TPU:1, one launch (start us, length us, event | category | flops | bytes accessed | tf_op | source)
XLA Modules:
  0.0 178.3 jit_solution(17253392555811810986)
XLA Ops:
  6.5 0.0 all-gather.2.cloned.1.call-start
  6.5 0.7 all-gather.2.cloned.1.call-update
  7.3 0.8 copy.25
  8.0 0.1 reshape.195
  8.1 0.1 convert_reduce_fusion
  8.2 0.1 select_reduce_fusion.1
  8.3 0.1 broadcast_in_dim.87
  8.4 0.1 reshape.196
  8.6 0.0 copy-start.1
  8.6 0.9 copy-done.1
  9.5 0.0 copy-start.2
  9.5 0.9 copy-done.2
  10.5 0.0 copy-start.3
  10.5 0.9 copy-done.3
  11.4 0.0 copy-start.6
  11.4 0.7 copy-done.6
  12.1 0.0 copy-start.7
  12.1 0.7 copy-done.7
  12.8 0.0 copy-start.8
  12.8 0.7 copy-done.8
  13.5 0.0 copy-start.9
  13.5 0.7 copy-done.9
  14.1 2.0 %attend.1 = bf16[64,1536]{1,0:T(8,128)(2,1)S(1)} custom-call(s32[2]{0:T(128)S(1)} %copy-done.9, s32[2]{0:T(128)S(1)} %copy-done.8, bf16[2,32,1536]{2,1,0:T(8,128)(2,1)S(1)} %copy-done.3, bf16[2,512,128]{2,1,0:T(8,128)(2,1)S(1)} %copy-done.1, bf16[2,512,128]{2,1,0:T(8,128)(2,1)S(1)} %copy-done.2, bf16[2,32,128]{2,1,0:T(8,128)(2,1)S(1)} %copy-done.6, ...), custom_call_target="tpu_custom_call" | custom-call | flops 213909504 | bytes 1048576 | tf_op jit(solution)/shard_map/attend/pallas_call | solution.py:69
  16.1 13.6 %all_gather.6 = bf16[256,1536]{1,0:T(8,128)(2,1)S(1)} all-gather(bf16[64,1536]{1,0:T(8,128)(2,1)S(1)} %attend.1), channel_id=1, replica_groups=mesh['y'=4,'z'=4,'c'=2,'x'=4] {'y'}, dimensions={0}, use_global_device_ids=true | all-gather | bytes 983040 | tf_op jit(solution)/shard_map/all_gather | solution.py:269
  29.7 0.0 copy-start.4
  29.7 0.0 copy-start.5
  29.7 14.3 %all-gather.2.cloned.1.call-done = bf16[1280,1536]{1,0:T(8,128)(2,1)} async-done(((bf16[160,1536]{1,0:T(8,128)(2,1)}), bf16[1280,1536]{1,0:T(8,128)(2,1)}) %all-gather.2.cloned.1.call-update) | async-done | bytes 3932176 | tf_op jit(solution)/shard_map/all_gather | solution.py:267
  44.0 4.2 %convolution_convert_fusion = bf16[256,1280]{1,0:T(8,128)(2,1)} fusion(bf16[256,1536]{1,0:T(8,128)(2,1)S(1)} %all_gather.6, bf16[1280,1536]{1,0:T(8,128)(2,1)} %all-gather.2.cloned.1.call-done), kind=kOutput, calls=%fused_computation | convolution fusion | flops 1006960640 | bytes 5373952 | tf_op jit(solution)/shard_map/dot_general | solution.py:26
  48.1 6.5 %all-to-all-start = ((bf16[16,16,1280]{2,1,0:T(8,128)(2,1)}), bf16[16,16,1280]{2,1,0:T(8,128)(2,1)S(1)}, u32[]{:S(2)}, u32[]{:S(2)}) async-start(bf16[16,16,1280]{2,1,0:T(8,128)(2,1)} %bitcast.1), calls=%async_computation | async-start | bytes 1310720 | tf_op jit(solution)/shard_map/all_to_all | solution.py:283
  54.7 0.3 fusion.place_ref
  55.0 11.9 %all-to-all-done.arrived_ref = bf16[16,16,1280]{2,1,0:T(8,128)(2,1)S(1)} async-done(((bf16[16,16,1280]{2,1,0:T(8,128)(2,1)}), bf16[16,16,1280]{2,1,0:T(8,128)(2,1)S(1)}, u32[]{:S(2)}, u32[]{:S(2)}) %all-to-all-start) | async-done | bytes 655392 | tf_op jit(solution)/shard_map/all_to_all | solution.py:283
  66.9 0.0 copy-done.4
  66.9 0.0 copy-done.5
  66.9 1.0 norm_place.1
  68.0 41.9 %all_to_all.15 = bf16[128,16,640]{2,1,0:T(8,128)(2,1)} all-to-all(bf16[128,16,640]{2,1,0:T(8,128)(2,1)S(1)} %bitcast.15), channel_id=1, replica_groups=mesh['y'=4,'z'=4,'c'=2,'x'=4] {'y','z','c','x'}, dimensions={0} | all-to-all | bytes 5242880 | tf_op jit(solution)/shard_map/all_to_all | solution.py:286
  109.8 18.4 %expert.1 = bf16[2048,640]{1,0:T(8,128)(2,1)} custom-call(bf16[2048,640]{1,0:T(8,128)(2,1)} %bitcast.18, bf16[5120,768]{1,0:T(8,128)(2,1)} %bitcast.19, bf16[5120,768]{1,0:T(8,128)(2,1)} %bitcast.20, bf16[768,5120]{1,0:T(8,128)(2,1)} %bitcast.21), custom_call_target="tpu_custom_call" | custom-call | tf_op jit(solution)/shard_map/expert/pallas_call | solution.py:179
  128.2 0.0 copy-start.11
  128.2 0.0 copy-start.10
  128.3 3.7 %all-to-all-start.2 = ((bf16[128,16,640]{2,1,0:T(8,128)(2,1)}), bf16[128,16,640]{2,1,0:T(8,128)(2,1)S(1)}, u32[]{:S(2)}, u32[]{:S(2)}) async-start(bf16[128,16,640]{2,1,0:T(8,128)(2,1)} %bitcast.17), calls=%async_computation.2 | async-start | bytes 5242880 | tf_op jit(solution)/shard_map/all_to_all | solution.py:291
  132.0 0.0 copy-done.11
  132.0 0.1 copy.26
  132.1 0.1 broadcast_in_dim.89
  132.1 0.1 select_reduce_fusion
  132.3 0.1 broadcast_in_dim.92
  132.4 0.1 reshape.201
  132.5 0.0 copy-done.10
  132.5 0.1 fusion.8
  132.6 0.1 copy.27
  132.7 1.0 select_convert_fusion
  133.7 35.0 %all-to-all-done.2 = bf16[128,16,640]{2,1,0:T(8,128)(2,1)S(1)} async-done(((bf16[128,16,640]{2,1,0:T(8,128)(2,1)}), bf16[128,16,640]{2,1,0:T(8,128)(2,1)S(1)}, u32[]{:S(2)}, u32[]{:S(2)}) %all-to-all-start.2) | async-done | bytes 2621472 | tf_op jit(solution)/shard_map/all_to_all | solution.py:291
  168.7 0.0 copy-start
  168.7 1.0 copy-done
  169.8 1.7 combine.1
  (7 shorter events, 0.1 us)
Async XLA Ops:
  6.5 37.4 %all-gather.2.cloned.1.call-start = ((), (), s32[]{:S(2)}) async-start(), calls=%async_computation.3 | async-start | bytes 4423680 | tf_op jit(solution)/shard_map/all_gather | solution.py:267
  8.6 1.0 copy-start.1
  9.5 0.9 copy-start.2
  10.5 0.9 copy-start.3
  11.4 0.7 copy-start.6
  12.1 0.7 copy-start.7
  12.8 0.7 copy-start.8
  13.5 0.7 copy-start.9
  29.7 37.2 %copy-start.4 = (bf16[16,5120]{1,0:T(8,128)(2,1)S(1)}, bf16[16,5120]{1,0:T(8,128)(2,1)}, u32[]{:S(2)}) copy-start(bf16[16,5120]{1,0:T(8,128)(2,1)} %residual_ref.1) | copy-start | bytes 491524
  29.7 37.2 %copy-start.5 = (f32[5120]{0:T(1024)S(1)}, f32[5120]{0:T(1024)}, u32[]{:S(2)}) copy-start(f32[5120]{0:T(1024)} %param.24) | copy-start | bytes 61444
  48.1 18.8 %all-to-all-start = ((bf16[16,16,1280]{2,1,0:T(8,128)(2,1)}), bf16[16,16,1280]{2,1,0:T(8,128)(2,1)S(1)}, u32[]{:S(2)}, u32[]{:S(2)}) async-start(bf16[16,16,1280]{2,1,0:T(8,128)(2,1)} %bitcast.1), calls=%async_computation | async-start | bytes 1310720 | tf_op jit(solution)/shard_map/all_to_all | solution.py:283
  128.2 3.7 %copy-start.11 = (f32[16,8]{0,1:T(8,128)S(1)}, f32[16,8]{0,1:T(8,128)}, u32[]{:S(2)}) copy-start(f32[16,8]{0,1:T(8,128)} %param.26) | copy-start | bytes 1540
  128.2 4.3 %copy-start.10 = (s32[2]{0:T(128)S(1)}, s32[2]{0:T(128)}, u32[]{:S(2)}) copy-start(s32[2]{0:T(128)} %counts.1) | copy-start | bytes 28
  128.3 40.5 %all-to-all-start.2 = ((bf16[128,16,640]{2,1,0:T(8,128)(2,1)}), bf16[128,16,640]{2,1,0:T(8,128)(2,1)S(1)}, u32[]{:S(2)}, u32[]{:S(2)}) async-start(bf16[128,16,640]{2,1,0:T(8,128)(2,1)} %bitcast.17), calls=%async_computation.2 | async-start | bytes 5242880 | tf_op jit(solution)/shard_map/all_to_all | solution.py:291
  168.7 1.0 copy-start
Sparse Core Ops, SparseCore 0:
  9.0 34.8 all-gather.1

commit v2 on v1

--- a/solution.py
+++ b/solution.py
@@ -12,7 +12,8 @@
 TOPK = 8
 CAP = 2
 LANES = 128
-SEG = 8
+AHEAD = 6
+SEG = 4
 AXES = ("y", "z", "c", "x")
 BF = jnp.bfloat16
 F32 = jnp.float32
@@ -30,7 +31,36 @@
     return [pl.BlockSpec(memory_space=pltpu.VMEM)] * n
 
 
-def attend_kernel(counts, lengths, q_ref, k_ref, v_ref, nk_ref, nv_ref, out_ref):
+def attend_kernel(
+    counts_hbm,
+    lengths_hbm,
+    q_hbm,
+    k_hbm,
+    v_hbm,
+    nk_hbm,
+    nv_hbm,
+    out_ref,
+    counts,
+    lengths,
+    q_ref,
+    k_ref,
+    v_ref,
+    nk_ref,
+    nv_ref,
+    sems,
+):
+    pairs = (
+        (q_hbm, q_ref),
+        (k_hbm, k_ref),
+        (nk_hbm, nk_ref),
+        (lengths_hbm, lengths),
+        (counts_hbm, counts),
+        (v_hbm, v_ref),
+        (nv_hbm, nv_ref),
+    )
+    copies = [pltpu.make_async_copy(a, b, sems.at[i]) for i, (a, b) in enumerate(pairs)]
+    for copy in copies:
+        copy.start()
     requests, slots, width = q_ref.shape
     heads = width // HEAD_DIM
     cached = k_ref.shape[1]
@@ -39,6 +69,8 @@
     slot = lax.broadcasted_iota(jnp.int32, (rows, slots), 0) % slots
     fresh = lax.broadcasted_iota(jnp.int32, (rows, slots), 1)
     position = lax.broadcasted_iota(jnp.int32, (rows, cached), 1)
+    for copy in copies:
+        copy.wait()
     for r in range(requests):
         q = jnp.concatenate(
             [q_ref[r, :, h * HEAD_DIM : (h + 1) * HEAD_DIM] for h in range(heads)], axis=0
@@ -66,17 +98,70 @@
 
 def attend(queries, cache_keys, cache_values, new_keys, new_values, counts, lengths):
     requests, slots, width = queries.shape
+    arrays = (queries, cache_keys, cache_values, new_keys, new_values)
     return pl.pallas_call(
         attend_kernel,
         out_shape=jax.ShapeDtypeStruct((requests * slots, width), BF),
-        in_specs=[pl.BlockSpec(memory_space=pltpu.SMEM)] * 2 + vmem(5),
+        in_specs=[pl.BlockSpec(memory_space=pl.ANY)] * 7,
         out_specs=pl.BlockSpec(memory_space=pltpu.VMEM),
-        compiler_params=pltpu.CompilerParams(vmem_limit_bytes=32 << 20),
+        scratch_shapes=[pltpu.SMEM((requests,), jnp.int32)] * 2
+        + [pltpu.VMEM(a.shape, a.dtype) for a in arrays]
+        + [pltpu.SemaphoreType.DMA((7,))],
+        compiler_params=pltpu.CompilerParams(vmem_limit_bytes=60 << 20),
         cost_estimate=pl.CostEstimate(
             flops=4 * 768 * 544 * 128, bytes_accessed=1 << 20, transcendentals=768 * 544
         ),
         name="attend",
-    )(counts, lengths, queries, cache_keys, cache_values, new_keys, new_values)
+    )(counts, lengths, *arrays)
+
+
+def project_kernel(tokens_hbm, *refs):
+    pieces, (out_ref, tokens, weight, sems) = refs[:-4], refs[-4:]
+    zs, cs = lax.axis_size("z"), lax.axis_size("c")
+    z, c = lax.axis_index("z"), lax.axis_index("c")
+    part = pieces[0].shape[0]
+    copies = [pltpu.make_async_copy(tokens_hbm, tokens, sems.at[zs * cs])]
+    for i, piece in enumerate(pieces):
+        home = lax.rem(z + zs - i // cs, zs) * cs + lax.rem(c + i, cs)
+        at = pl.ds(pl.multiple_of(home * part, part), part)
+        copies.append(pltpu.make_async_copy(piece, weight.at[at, :], sems.at[i]))
+    for copy in copies:
+        copy.start()
+    for copy in copies:
+        copy.wait()
+    tile = 256
+    for j in range(out_ref.shape[1] // tile):
+        at = slice(j * tile, (j + 1) * tile)
+        out_ref[:, at] = dot_t(tokens[...], weight[at, :]).astype(BF)
+
+
+def project(tokens, o_weight, ready):
+    zs = lax.axis_size("z")
+    swap = [(0, 1), (1, 0)]
+    own = o_weight.T
+    along = [own] + [
+        lax.ppermute(own, "z", [(i, (i + k) % zs) for i in range(zs)]) for k in range(1, zs)
+    ]
+    *along, tokens, ready = lax.optimization_barrier((*along, tokens, ready))
+    pieces = []
+    for piece in along:
+        pieces += [piece, lax.ppermute(piece, "c", swap)]
+    part, depth = own.shape
+    columns = part * len(pieces)
+    call = pl.pallas_call(
+        project_kernel,
+        out_shape=jax.ShapeDtypeStruct((tokens.shape[0], columns), BF),
+        in_specs=[pl.BlockSpec(memory_space=pl.ANY)] * (1 + len(pieces)),
+        out_specs=pl.BlockSpec(memory_space=pltpu.VMEM),
+        scratch_shapes=[
+            pltpu.VMEM(tokens.shape, BF),
+            pltpu.VMEM((columns, depth), BF),
+            pltpu.SemaphoreType.DMA((len(pieces) + 1,)),
+        ],
+        compiler_params=pltpu.CompilerParams(vmem_limit_bytes=60 << 20),
+        name="project",
+    )
+    return call(tokens, *pieces), ready
 
 
 def norm_kernel(arrived_ref, residual_ref, gain_ref, place_ref, hidden_ref, out_ref):
@@ -126,44 +211,47 @@
 
 
 def expert_kernel(
-    x_ref, gate_hbm, up_hbm, down_hbm, out_ref, stage, gate, up, down, inner, sems
+    x_ref, gate_hbm, up_hbm, down_hbm, out_ref, stage, inner, gate, up, down, sems
 ):
     rows = x_ref.shape[0] // SEG
     seg = x_ref.shape[1]
-    half = gate.shape[1]
     lanes = seg // LANES
-
-    def piece(kind, s):
+    copies = []
+    for s in range(SEG):
         at = pl.ds(s * seg, seg)
-        if kind == 0:
-            return pltpu.make_async_copy(gate_hbm.at[at, :], gate.at[at, :], sems.at[0, s])
-        if kind == 1:
-            return pltpu.make_async_copy(up_hbm.at[at, :], up.at[at, :], sems.at[1, s])
-        return pltpu.make_async_copy(down_hbm.at[:, at], down.at[:, at], sems.at[2, s])
-
+        copies.append(pltpu.make_async_copy(gate_hbm.at[at, :], gate.at[at, :], sems.at[0, s]))
+        copies.append(pltpu.make_async_copy(up_hbm.at[at, :], up.at[at, :], sems.at[1, s]))
     for s in range(SEG):
-        piece(0, s).start()
-        piece(1, s).start()
-    for s in range(SEG):
-        piece(2, s).start()
+        at = pl.ds(s * seg, seg)
+        copies.append(pltpu.make_async_copy(down_hbm.at[:, at], down.at[:, at], sems.at[2, s]))
+
+    def need(i):
+        copies[i].wait()
+        if i + AHEAD < len(copies):
+            copies[i + AHEAD].start()
+
+    for copy in copies[:AHEAD]:
+        copy.start()
     tile = 256
     for i in range(x_ref.shape[0] // tile):
         at = pl.ds(i * tile, tile)
         for k in range(lanes):
             stage[k, at, :] = x_ref[at, k * LANES : (k + 1) * LANES].astype(F32)
-    gate_sum = jnp.zeros((rows, half), F32)
-    up_sum = jnp.zeros((rows, half), F32)
+    gate_sum = up_sum = None
     for s in range(SEG):
+        at = pl.ds(s * seg, seg)
         x = jnp.concatenate(
             [stage[k, pl.ds(s, rows, stride=SEG), :].astype(BF) for k in range(lanes)], axis=1
         )
-        piece(0, s).wait()
-        gate_sum = gate_sum + dot(x, gate[pl.ds(s * seg, seg), :])
-        piece(1, s).wait()
-        up_sum = up_sum + dot(x, up[pl.ds(s * seg, seg), :])
+        need(2 * s)
+        gate_part = dot(x, gate[at, :])
+        need(2 * s + 1)
+        up_part = dot(x, up[at, :])
+        gate_sum = gate_part if s == 0 else gate_sum + gate_part
+        up_sum = up_part if s == 0 else up_sum + up_part
     inner[...] = (gate_sum / (1.0 + jnp.exp(-gate_sum)) * up_sum).astype(BF)
     for s in range(SEG):
-        piece(2, s).wait()
+        need(2 * SEG + s)
         result = dot(inner[...], down[:, pl.ds(s * seg, seg)])
         for k in range(lanes):
             stage[k, pl.ds(s, rows, stride=SEG), :] = result[:, k * LANES : (k + 1) * LANES]
@@ -183,13 +271,13 @@
         out_specs=pl.BlockSpec(memory_space=pltpu.VMEM),
         scratch_shapes=[
             pltpu.VMEM((seg // LANES, count, LANES), F32),
+            pltpu.VMEM((count // SEG, half), BF),
             pltpu.VMEM((width, half), BF),
             pltpu.VMEM((width, half), BF),
             pltpu.VMEM((half, width), BF),
-            pltpu.VMEM((count // SEG, half), BF),
             pltpu.SemaphoreType.DMA((3, SEG)),
         ],
-        compiler_params=pltpu.CompilerParams(vmem_limit_bytes=52 << 20),
+        compiler_params=pltpu.CompilerParams(vmem_limit_bytes=44 << 20),
         name="expert",
     )(rows, gate, up, down)
 
@@ -264,7 +352,6 @@
     requests, slots, _ = queries.shape
     rows, width = residual.shape
     experts = math.prod(lax.axis_size(a) for a in AXES)
-    weight = lax.all_gather(o_weight.T, ("z", "c"), axis=0, tiled=True)
     attended = attend(queries, cache_keys, cache_values, new_keys, new_values, counts, lengths)
     tokens = lax.all_gather(attended, "y", axis=0, tiled=True)
     place, high, low = routing(expert_ids, route_weights, experts)
@@ -278,7 +365,7 @@
         axis=1,
     )
     live = (token_index % slots < count_of).astype(jnp.int32)[:, None]
-    partial = dot_t(tokens, weight).astype(BF)
+    partial, (place, high, low, live) = project(tokens, o_weight, (place, high, low, live))
     partial = partial.reshape(-1, rows, partial.shape[1])
     arrived = lax.all_to_all(partial, ("y", "x"), split_axis=0, concat_axis=0, tiled=True)
     hidden, outgoing = norm_and_place(arrived, residual, norm_gain[None, :], place)

time: 179 us -> 154 us (0.86)
  blocking collectives: 55.4 us -> 114 us
  waiting for transfers between devices: 61.9 us -> 6.06 us
  between operations: 13.5 us -> 0.16 us
  local copies, waits for them, and re-layouts: 8.14 us -> 3 us
  matrix products: 4.17 us -> 0 us
  starting transfers between devices: 10.2 us -> 6.89 us
    all_to_all x0 -> x2, blocking collectives: none -> 58.9 us  [the longest x1 39.8 us: per_device(): lax.all_to_all(results, AXES, split_axis=0, concat_axis=0, tiled=True)]
    all_to_all x2 -> x0, waiting for transfers between devices: 46.9 us -> none  [the longest x1 35 us: per_device(): lax.all_to_all(results, AXES, split_axis=0, concat_axis=0, tiled=True)]
    all_gather x1 -> x0, waiting for transfers between devices: 14.3 us -> none  [per_device(): weight = lax.all_gather(o_weight.T, ('z', 'c'), axis=0, tiled=True)]
    all_to_all x2 -> x0, starting transfers between devices: 10.2 us -> none  [the longest x1 6.53 us: per_device(): lax.all_to_all(partial, ('y', 'x'), split_axis=0, concat_axis=0, tiled=True)]
    ppermute x0 -> x7, starting transfers between devices: none -> 6.89 us  [the longest x3 5.29 us: project(): lax.ppermute(own, 'z', [(i, (i + k) % zs) for i in range(zs)])]
    pallas_call x1, Pallas kernels: 18.4 us -> 12.2 us  [apply_expert(): pl.pallas_call(expert_kernel, out_shape=jax.ShapeDtypeStruct((count, seg)...]
    ppermute x0 -> x7, waiting for transfers between devices: none -> 6.06 us  [the longest x3 3.07 us: project(): lax.ppermute(own, 'z', [(i, (i + k) % zs) for i in range(zs)])]
    unnamed x26 -> x20, local copies, waits for them, and re-layouts: 7.46 us -> 2.32 us
  transfers between devices with their start and end apart: 3 -> 7, of which waited for: 3 -> 4; matrix products, arithmetic and copies ran while one was open for 2% -> 2% of each run, Pallas kernels for 1% -> 2%
where the time goes in v2:
time: 154 us
  blocking collectives  114 us (74%)
  Pallas kernels  22.7 us (15%)
  starting transfers between devices  6.89 us (4%)
  waiting for transfers between devices  6.06 us (4%)
  local copies, waits for them, and re-layouts  3 us (2%)
    all_to_all x1, blocking collectives, per_device(): lax.all_to_all(outgoing, AXES, split_axis=0, concat_axis=0, tiled=True)  41 us
    all_to_all x1, blocking collectives, per_device(): lax.all_to_all(results, AXES, split_axis=0, concat_axis=0, tiled=True)  39.8 us
    all_to_all x1, blocking collectives, per_device(): lax.all_to_all(partial, ('y', 'x'), split_axis=0, concat_axis=0, tiled=True)  19.1 us
    all_gather x1, blocking collectives, per_device(): tokens = lax.all_gather(attended, 'y', axis=0, tiled=True)  14 us
    pallas_call x1, Pallas kernels, apply_expert(): pl.pallas_call(expert_kernel, out_shape=jax.ShapeDtypeStruct((count, seg)...  12.2 us
    ppermute x3, starting transfers between devices, project(): lax.ppermute(own, 'z', [(i, (i + k) % zs) for i in range(zs)])  5.29 us
    pallas_call x1, Pallas kernels, project(): return (call(tokens, *pieces), ready)  4.47 us
    pallas_call x1, Pallas kernels, attend(): pl.pallas_call(attend_kernel, out_shape=jax.ShapeDtypeStruct((requests *...  3.32 us
  transfers between devices with their start and end apart: 7, of which 4 were waited for; matrix products, arithmetic and copies ran while one was open for 2% of the time, Pallas kernels for 2%

profile of v2, /device:TPU:1, one launch (start us, length us, event | category | flops | bytes accessed | tf_op | source)
XLA Modules:
  0.0 154.1 jit_solution(14116479996514116073)
XLA Ops:
  0.0 0.0 copy-start.2
  0.0 4.6 %collective-permute-start.2 = (bf16[160,1536]{1,0:T(8,128)(2,1)}, bf16[160,1536]{1,0:T(8,128)(2,1)S(1)}, u32[]{:S(2)}, u32[]{:S(2)}) collective-permute-start(bf16[160,1536]{1,0:T(8,128)(2,1)} %bitcast.20), channel_id=1, source_target_pairs={{0,24},{8,0},{16,8},{24,16},{1,25},{9,1},{17,9},{25,17},{2,26},{10... | collective-permute-start | bytes 1474568 | tf_op jit(solution)/shard_map/ppermute | solution.py:143
  4.6 0.0 collective-permute-start.1
  4.6 0.7 collective-permute-start
  5.3 0.7 fusion.14
  6.0 0.1 copy.24
  6.1 0.8 copy.22
  6.9 0.1 reshape.194
  7.0 0.1 convert_reduce_fusion
  7.1 0.1 select_reduce_fusion.1
  7.2 0.8 copy.23
  8.0 0.1 broadcast_in_dim.88
  8.1 0.1 select_reduce_fusion
  8.2 0.1 broadcast_in_dim.91
  8.3 0.1 reshape.196
  8.4 0.1 broadcast_in_dim.86
  8.5 0.1 reshape.195
  8.7 0.2 fusion.place_ref
  8.9 3.3 %attend.1 = bf16[64,1536]{1,0:T(8,128)(2,1)} custom-call(s32[2]{0:T(128)} %counts_hbm.1, s32[2]{0:T(128)} %lengths_hbm.1, bf16[2,32,1536]{2,1,0:T(8,128)(2,1)} %q_hbm.1, bf16[2,512,128]{2,1,0:T(8,128)(2,1)} %k_hbm.1, bf16[2,512,128]{2,1,0:T(8,128)(2,1)} %v_hbm.1, bf16[2,32,128]{2,1,0:T(8,128)(2,1)} %nk_hbm.1, bf16[2,32,128]{2,1,0:T(8,128)(2,1)} %nv_hbm.1), custom_call_target="tpu_custom_call" | custom-call | flops 213909504 | bytes 1048576 | tf_op jit(solution)/shard_map/attend/pallas_call | solution.py:102
  12.3 14.0 %all_gather.3.tokens_hbm = bf16[256,1536]{1,0:T(8,128)(2,1)} all-gather(bf16[64,1536]{1,0:T(8,128)(2,1)} %attend.1), channel_id=1, replica_groups=mesh['y'=4,'z'=4,'c'=2,'x'=4] {'y'}, dimensions={0}, use_global_device_ids=true | all-gather | bytes 983040 | tf_op jit(solution)/shard_map/all_gather | solution.py:356
  26.3 0.0 collective-permute-done.2.refs_6_
  26.3 0.0 copy-start.3
  26.3 0.0 collective-permute-done.1.refs_4_
  26.3 0.0 copy-start.4
  26.3 3.1 %collective-permute-done.refs_2_ = bf16[160,1536]{1,0:T(8,128)(2,1)S(1)} collective-permute-done((bf16[160,1536]{1,0:T(8,128)(2,1)}, bf16[160,1536]{1,0:T(8,128)(2,1)S(1)}, u32[]{:S(2)}, u32[]{:S(2)}) %collective-permute-start) | collective-permute-done | bytes 491552 | tf_op jit(solution)/shard_map/ppermute | solution.py:143
  29.3 0.0 copy-start.5
  29.3 0.0 copy-done.2
  29.4 0.0 copy-start
  29.4 0.0 copy-start.1
  29.4 1.0 collective-permute-start.3
  30.4 0.1 collective-permute-start.4
  30.4 0.4 collective-permute-start.5
  30.9 0.1 collective-permute-start.6
  31.0 0.9 collective-permute-done.3.refs_1_
  31.8 0.0 copy-start.6
  31.8 1.4 collective-permute-done.4.refs_3_
  33.3 0.0 copy-start.7
  33.3 0.7 collective-permute-done.5.refs_5_
  34.0 0.0 copy-start.8
  34.0 0.8 copy-done.8
  34.7 0.0 collective-permute-done.6.refs_7_
  34.7 0.0 copy-done.3
  34.7 0.0 copy-done.4
  34.7 0.0 copy-done.5
  34.8 0.0 copy-done.6
  34.8 0.0 copy-done.7
  34.8 4.5 %project.1 = bf16[256,1280]{1,0:T(8,128)(2,1)} custom-call(bf16[256,1536]{1,0:T(8,128)(2,1)} %all_gather.3.tokens_hbm, bf16[160,1536]{1,0:T(8,128)(2,1)} %bitcast.23, bf16[160,1536]{1,0:T(8,128)(2,1)} %copy-done.6, bf16[160,1536]{1,0:T(8,128)(2,1)} %copy-done.5, bf16[160,1536]{1,0:T(8,128)(2,1)} %copy-done.7, bf16[160,1536]{1,0:T(8,128)(2,1)} %copy-done.4, ...), custom_call_target="tpu_custom_call" | custom-call | tf_op jit(solution)/shard_map/project/pallas_call | solution.py:164
  39.2 19.1 %all_to_all.15.arrived_ref = bf16[16,16,1280]{2,1,0:T(8,128)(2,1)S(1)} all-to-all(bf16[16,16,1280]{2,1,0:T(8,128)(2,1)} %bitcast.19), channel_id=1, replica_groups=mesh['y'=4,'z'=4,'c'=2,'x'=4] {'y','x'}, dimensions={0} | all-to-all | bytes 1310720 | tf_op jit(solution)/shard_map/all_to_all | solution.py:370
  58.4 0.0 copy-done
  58.4 0.0 copy-done.1
  58.4 1.0 norm_place.1
  59.4 41.0 %all_to_all.16 = bf16[128,8,1280]{2,1,0:T(8,128)(2,1)S(1)} all-to-all(bf16[128,8,1280]{2,1,0:T(8,128)(2,1)S(1)} %bitcast.14), channel_id=1, replica_groups=mesh['y'=4,'z'=4,'c'=2,'x'=4] {'y','z','c','x'}, dimensions={0} | all-to-all | bytes 5242880 | tf_op jit(solution)/shard_map/all_to_all | solution.py:373
  100.4 12.2 %expert.1 = bf16[1024,1280]{1,0:T(8,128)(2,1)S(1)} custom-call(bf16[1024,1280]{1,0:T(8,128)(2,1)S(1)} %bitcast.11, bf16[5120,768]{1,0:T(8,128)(2,1)} %bitcast.16, bf16[5120,768]{1,0:T(8,128)(2,1)} %bitcast.17, bf16[768,5120]{1,0:T(8,128)(2,1)} %bitcast.18), custom_call_target="tpu_custom_call" | custom-call | tf_op jit(solution)/shard_map/expert/pallas_call | solution.py:267
  112.6 39.8 %all_to_all.17 = bf16[128,8,1280]{2,1,0:T(8,128)(2,1)S(1)} all-to-all(bf16[128,8,1280]{2,1,0:T(8,128)(2,1)S(1)} %bitcast.12), channel_id=1, replica_groups=mesh['y'=4,'z'=4,'c'=2,'x'=4] {'y','z','c','x'}, dimensions={0} | all-to-all | bytes 5242880 | tf_op jit(solution)/shard_map/all_to_all | solution.py:378
  152.4 1.7 %combine.1 = bf16[16,5120]{1,0:T(8,128)(2,1)} custom-call(bf16[1024,1280]{1,0:T(8,128)(2,1)S(1)} %bitcast.13, bf16[64,1024]{1,0:T(8,128)(2,1)S(1)} %get-tuple-element.23.high_ref, bf16[64,1024]{1,0:T(8,128)(2,1)S(1)} %get-tuple-element.24.low_ref, f32[16,5120]{1,0:T(8,128)S(1)} %get-tuple-element.25.hidden_ref, s32[16,1]{1,0:T(8,128)S(1)} %fusion.7.live_ref), custom_call_target="tpu_custom_call" | custom-call | tf_op jit(solution)/shard_map/combine/pallas_call | solution.py:298
  (7 shorter events, 0.1 us)
Async XLA Ops:
  0.0 29.3 %copy-start.2 = (bf16[1536,160]{0,1:T(8,128)(2,1)S(1)}, bf16[1536,160]{0,1:T(8,128)(2,1)}, u32[]{:S(2)}) copy-start(bf16[1536,160]{0,1:T(8,128)(2,1)} %param.23) | copy-start | bytes 1474564
  0.0 26.3 %collective-permute-start.2 = (bf16[160,1536]{1,0:T(8,128)(2,1)}, bf16[160,1536]{1,0:T(8,128)(2,1)S(1)}, u32[]{:S(2)}, u32[]{:S(2)}) collective-permute-start(bf16[160,1536]{1,0:T(8,128)(2,1)} %bitcast.20), channel_id=1, source_target_pairs={{0,24},{8,0},{16,8},{24,16},{1,25},{9,1},{17,9},{25,17},{2,26},{10... | collective-permute-start | bytes 1474568 | tf_op jit(solution)/shard_map/ppermute | solution.py:143
  4.6 21.7 %collective-permute-start.1 = (bf16[160,1536]{1,0:T(8,128)(2,1)}, bf16[160,1536]{1,0:T(8,128)(2,1)S(1)}, u32[]{:S(2)}, u32[]{:S(2)}) collective-permute-start(bf16[160,1536]{1,0:T(8,128)(2,1)} %bitcast.21), channel_id=1, source_target_pairs={{0,16},{8,24},{16,0},{24,8},{1,17},{9,25},{17,1},{25,9},{2,18},{10... | collective-permute-start | bytes 1474568 | tf_op jit(solution)/shard_map/ppermute | solution.py:143
  4.6 24.8 %collective-permute-start = (bf16[160,1536]{1,0:T(8,128)(2,1)}, bf16[160,1536]{1,0:T(8,128)(2,1)S(1)}, u32[]{:S(2)}, u32[]{:S(2)}) collective-permute-start(bf16[160,1536]{1,0:T(8,128)(2,1)} %bitcast.22), channel_id=1, source_target_pairs={{0,8},{8,16},{16,24},{24,0},{1,9},{9,17},{17,25},{25,1},{2,10},{10... | collective-permute-start | bytes 1474568 | tf_op jit(solution)/shard_map/ppermute | solution.py:143
  26.3 8.5 %copy-start.3 = (bf16[160,1536]{1,0:T(8,128)(2,1)}, bf16[160,1536]{1,0:T(8,128)(2,1)S(1)}, u32[]{:S(2)}) copy-start(bf16[160,1536]{1,0:T(8,128)(2,1)S(1)} %collective-permute-done.2.refs_6_) | copy-start | bytes 1474564
  26.3 8.5 %copy-start.4 = (bf16[160,1536]{1,0:T(8,128)(2,1)}, bf16[160,1536]{1,0:T(8,128)(2,1)S(1)}, u32[]{:S(2)}) copy-start(bf16[160,1536]{1,0:T(8,128)(2,1)S(1)} %collective-permute-done.1.refs_4_) | copy-start | bytes 1474564
  29.3 5.4 %copy-start.5 = (bf16[160,1536]{1,0:T(8,128)(2,1)}, bf16[160,1536]{1,0:T(8,128)(2,1)S(1)}, u32[]{:S(2)}) copy-start(bf16[160,1536]{1,0:T(8,128)(2,1)S(1)} %collective-permute-done.refs_2_) | copy-start | bytes 1474564
  29.4 29.0 %copy-start = (bf16[16,5120]{1,0:T(8,128)(2,1)S(1)}, bf16[16,5120]{1,0:T(8,128)(2,1)}, u32[]{:S(2)}) copy-start(bf16[16,5120]{1,0:T(8,128)(2,1)} %residual_ref.1) | copy-start | bytes 491524
  29.4 29.0 %copy-start.1 = (f32[5120]{0:T(1024)S(1)}, f32[5120]{0:T(1024)}, u32[]{:S(2)}) copy-start(f32[5120]{0:T(1024)} %param.24) | copy-start | bytes 61444
  29.4 2.5 %collective-permute-start.3 = (bf16[160,1536]{1,0:T(8,128)(2,1)S(1)}, bf16[160,1536]{1,0:T(8,128)(2,1)S(1)}, u32[]{:S(2)}, u32[]{:S(2)}) collective-permute-start(bf16[160,1536]{1,0:T(8,128)(2,1)S(1)} %bitcast.24), channel_id=1, source_target_pairs={{0,4},{4,0},{1,5},{5,1},{2,6},{6,2},{3,7},{7,3},{8,12},{12,8},{9,1... | collective-permute-start | bytes 1474568 | tf_op jit(solution)/shard_map/ppermute | solution.py:148
  30.4 2.9 %collective-permute-start.4 = (bf16[160,1536]{1,0:T(8,128)(2,1)S(1)}, bf16[160,1536]{1,0:T(8,128)(2,1)S(1)}, u32[]{:S(2)}, u32[]{:S(2)}) collective-permute-start(bf16[160,1536]{1,0:T(8,128)(2,1)S(1)} %collective-permute-done.refs_2_), channel_id=1, source_target_pairs={{0,4},{4,0},{1,5},{5,1},{2,6},{6,2},{3,7},{7,3},{8,12},{12,8},{9,1... | collective-permute-start | bytes 1474568 | tf_op jit(solution)/shard_map/ppermute | solution.py:148
  30.4 3.5 %collective-permute-start.5 = (bf16[160,1536]{1,0:T(8,128)(2,1)S(1)}, bf16[160,1536]{1,0:T(8,128)(2,1)S(1)}, u32[]{:S(2)}, u32[]{:S(2)}) collective-permute-start(bf16[160,1536]{1,0:T(8,128)(2,1)S(1)} %collective-permute-done.1.refs_4_), channel_id=1, source_target_pairs={{0,4},{4,0},{1,5},{5,1},{2,6},{6,2},{3,7},{7,3},{8,12},{12,8},{9,1... | collective-permute-start | bytes 1474568 | tf_op jit(solution)/shard_map/ppermute | solution.py:148
  30.9 3.9 %collective-permute-start.6 = (bf16[160,1536]{1,0:T(8,128)(2,1)S(1)}, bf16[160,1536]{1,0:T(8,128)(2,1)}, u32[]{:S(2)}, u32[]{:S(2)}) collective-permute-start(bf16[160,1536]{1,0:T(8,128)(2,1)S(1)} %collective-permute-done.2.refs_6_), channel_id=1, source_target_pairs={{0,4},{4,0},{1,5},{5,1},{2,6},{6,2},{3,7},{7,3},{8,12},{12,8},{9,1... | collective-permute-start | bytes 1474568 | tf_op jit(solution)/shard_map/ppermute | solution.py:148
  31.8 2.9 %copy-start.6 = (bf16[160,1536]{1,0:T(8,128)(2,1)}, bf16[160,1536]{1,0:T(8,128)(2,1)S(1)}, u32[]{:S(2)}) copy-start(bf16[160,1536]{1,0:T(8,128)(2,1)S(1)} %collective-permute-done.3.refs_1_) | copy-start | bytes 1474564
  33.3 1.5 copy-start.7
  34.0 0.8 copy-start.8

commit v3 on v2

--- a/solution.py
+++ b/solution.py
@@ -1,3 +1,4 @@
+import functools
 import math
 
 import jax
@@ -115,66 +116,78 @@
     )(counts, lengths, *arrays)
 
 
-def project_kernel(tokens_hbm, *refs):
+def project_kernel(homes, near_hbm, across_hbm, *refs):
     pieces, (out_ref, tokens, weight, sems) = refs[:-4], refs[-4:]
-    zs, cs = lax.axis_size("z"), lax.axis_size("c")
-    z, c = lax.axis_index("z"), lax.axis_index("c")
+    z, zs, c = lax.axis_index("z"), lax.axis_size("z"), lax.axis_index("c")
     part = pieces[0].shape[0]
-    copies = [pltpu.make_async_copy(tokens_hbm, tokens, sems.at[zs * cs])]
-    for i, piece in enumerate(pieces):
-        home = lax.rem(z + zs - i // cs, zs) * cs + lax.rem(c + i, cs)
+    rows = near_hbm.shape[0]
+    copies = []
+    for i, (block, home) in enumerate(((near_hbm, c), (across_hbm, 1 - c))):
+        at = pl.ds(pl.multiple_of(home * rows, rows), rows)
+        copies.append(pltpu.make_async_copy(block, tokens.at[at, :], sems.at[len(pieces) + i]))
+    for i, (piece, back) in enumerate(zip(pieces, homes)):
+        home = lax.rem(z + zs - back, zs)
         at = pl.ds(pl.multiple_of(home * part, part), part)
         copies.append(pltpu.make_async_copy(piece, weight.at[at, :], sems.at[i]))
     for copy in copies:
         copy.start()
     for copy in copies:
         copy.wait()
-    tile = 256
-    for j in range(out_ref.shape[1] // tile):
-        at = slice(j * tile, (j + 1) * tile)
+    columns = out_ref.shape[1]
+    for j in range(0, columns, 256):
+        at = slice(j, min(j + 256, columns))
         out_ref[:, at] = dot_t(tokens[...], weight[at, :]).astype(BF)
 
 
-def project(tokens, o_weight, ready):
+def project(attended, o_weight, route):
     zs = lax.axis_size("z")
-    swap = [(0, 1), (1, 0)]
     own = o_weight.T
-    along = [own] + [
+    along = [
         lax.ppermute(own, "z", [(i, (i + k) % zs) for i in range(zs)]) for k in range(1, zs)
     ]
-    *along, tokens, ready = lax.optimization_barrier((*along, tokens, ready))
-    pieces = []
-    for piece in along:
-        pieces += [piece, lax.ppermute(piece, "c", swap)]
+    near = lax.all_gather(attended, "y", axis=0, tiled=True)
+    across = lax.ppermute(near, "c", [(0, 1), (1, 0)])
+    ready = route(near)
+    *along, near, across, ready = lax.optimization_barrier((*along, near, across, ready))
+    pieces = [own, *along]
+    rows = 2 * near.shape[0]
     part, depth = own.shape
-    columns = part * len(pieces)
+    columns = part * zs
     call = pl.pallas_call(
-        project_kernel,
-        out_shape=jax.ShapeDtypeStruct((tokens.shape[0], columns), BF),
-        in_specs=[pl.BlockSpec(memory_space=pl.ANY)] * (1 + len(pieces)),
+        functools.partial(project_kernel, tuple(range(zs))),
+        out_shape=jax.ShapeDtypeStruct((rows, columns), BF),
+        in_specs=[pl.BlockSpec(memory_space=pl.ANY)] * (2 + len(pieces)),
         out_specs=pl.BlockSpec(memory_space=pltpu.VMEM),
         scratch_shapes=[
-            pltpu.VMEM(tokens.shape, BF),
+            pltpu.VMEM((rows, depth), BF),
             pltpu.VMEM((columns, depth), BF),
-            pltpu.SemaphoreType.DMA((len(pieces) + 1,)),
+            pltpu.SemaphoreType.DMA((len(pieces) + 2,)),
         ],
         compiler_params=pltpu.CompilerParams(vmem_limit_bytes=60 << 20),
         name="project",
     )
-    return call(tokens, *pieces), ready
-
-
-def norm_kernel(arrived_ref, residual_ref, gain_ref, place_ref, hidden_ref, out_ref):
-    blocks, rows, part = arrived_ref.shape
+    return call(near, across, *pieces), ready
+
+
+def norm_kernel(hops, arrived_ref, residual_ref, gain_ref, place_ref, hidden_ref, out_ref):
+    groups, splits, halves, rows, parts, part = hops
     width = residual_ref.shape[1]
-    groups = width // part
-    splits = blocks // groups
     square = jnp.zeros((rows, 1), F32)
+    span = parts * part
     for g in range(groups):
-        total = residual_ref[:, g * part : (g + 1) * part].astype(F32)
-        for k in range(splits):
-            total = total + arrived_ref[g * splits + k].astype(F32)
-        hidden_ref[:, g * part : (g + 1) * part] = total
+        sums = []
+        for h in range(halves):
+            total = jnp.zeros((rows, span), F32)
+            for k in range(splits):
+                total = total + arrived_ref[(h * groups + g) * splits + k].astype(F32)
+            sums.append(total)
+        total = jnp.concatenate(
+            [sums[h][:, z * part : (z + 1) * part] for z in range(parts) for h in range(halves)],
+            axis=1,
+        )
+        at = slice(g * halves * span, (g + 1) * halves * span)
+        total = total + residual_ref[:, at].astype(F32)
+        hidden_ref[:, at] = total
         square = square + jnp.sum(total * total, axis=1, keepdims=True)
     factor = lax.rsqrt(square / width + 1e-05)
     seg = width // SEG
@@ -197,8 +210,10 @@
 
 def norm_and_place(arrived, residual, gain, place):
     rows, width = residual.shape
+    ys, xs, cs, zs = (lax.axis_size(a) for a in ("y", "x", "c", "z"))
+    hops = (ys, xs, cs, rows, zs, arrived.shape[2] // zs)
     return pl.pallas_call(
-        norm_kernel,
+        functools.partial(norm_kernel, hops),
         out_shape=(
             jax.ShapeDtypeStruct((rows, width), F32),
             jax.ShapeDtypeStruct((place.shape[0], width // SEG), BF),
@@ -282,11 +297,12 @@
     )(rows, gate, up, down)
 
 
-def combine_kernel(back_ref, high_ref, low_ref, hidden_ref, live_ref, out_ref):
+def combine_kernel(back_ref, shares_ref, hidden_ref, live_ref, out_ref):
     rows, width = hidden_ref.shape
     seg = width // SEG
-    back = back_ref[...]
-    mixed = dot(high_ref[...], back) + dot(low_ref[...], back)
+    half = SEG * rows
+    mixed = dot(shares_ref[...], back_ref[...])
+    mixed = mixed[:half] + mixed[half:]
     live = live_ref[...] > 0
     for s in range(SEG):
         at = slice(s * seg, (s + 1) * seg)
@@ -294,15 +310,15 @@
         out_ref[:, at] = jnp.where(live, total, 0.0).astype(BF)
 
 
-def combine(back, high, low, hidden, live):
+def combine(back, shares, hidden, live):
     return pl.pallas_call(
         combine_kernel,
         out_shape=jax.ShapeDtypeStruct(hidden.shape, BF),
-        in_specs=vmem(5),
+        in_specs=vmem(4),
         out_specs=pl.BlockSpec(memory_space=pltpu.VMEM),
         compiler_params=pltpu.CompilerParams(vmem_limit_bytes=32 << 20),
         name="combine",
-    )(back, high, low, hidden, live)
+    )(back, shares, hidden, live)
 
 
 def routing(expert_ids, route_weights, experts):
@@ -325,11 +341,10 @@
     high = lax.reduce_precision(weight_line, 8, 7)
     low = weight_line - high
     here = spot[:, None] == key[None, :]
-    return (
-        place,
-        jnp.where(here, high[None, :], 0.0).astype(BF),
-        jnp.where(here, low[None, :], 0.0).astype(BF),
-    )
+    shares = jnp.concatenate(
+        [jnp.where(here, part[None, :], 0.0).astype(BF) for part in (high, low)], axis=0
+    )
+    return place, shares
 
 
 def per_device(
@@ -353,8 +368,6 @@
     rows, width = residual.shape
     experts = math.prod(lax.axis_size(a) for a in AXES)
     attended = attend(queries, cache_keys, cache_values, new_keys, new_values, counts, lengths)
-    tokens = lax.all_gather(attended, "y", axis=0, tiled=True)
-    place, high, low = routing(expert_ids, route_weights, experts)
     token_index = lax.axis_index("x") * rows + jnp.arange(rows, dtype=jnp.int32)
     count_of = jnp.sum(
         jnp.where(
@@ -365,9 +378,14 @@
         axis=1,
     )
     live = (token_index % slots < count_of).astype(jnp.int32)[:, None]
-    partial, (place, high, low, live) = project(tokens, o_weight, (place, high, low, live))
+
+    def route(after):
+        ids, weights, _ = lax.optimization_barrier((expert_ids, route_weights, after))
+        return (*routing(ids, weights, experts), live)
+
+    partial, (place, shares, live) = project(attended, o_weight, route)
     partial = partial.reshape(-1, rows, partial.shape[1])
-    arrived = lax.all_to_all(partial, ("y", "x"), split_axis=0, concat_axis=0, tiled=True)
+    arrived = lax.all_to_all(partial, ("c", "y", "x"), split_axis=0, concat_axis=0, tiled=True)
     hidden, outgoing = norm_and_place(arrived, residual, norm_gain[None, :], place)
     outgoing = outgoing.reshape(experts, CAP * SEG, width // SEG)
     received = lax.all_to_all(outgoing, AXES, split_axis=0, concat_axis=0, tiled=True)
@@ -376,7 +394,7 @@
     )
     results = results.reshape(experts, CAP * SEG, width // SEG)
     back = lax.all_to_all(results, AXES, split_axis=0, concat_axis=0, tiled=True)
-    return combine(back.reshape(-1, width // SEG), high, low, hidden, live)
+    return combine(back.reshape(-1, width // SEG), shares, hidden, live)
 
 
 def solution(mesh):

time: 154 us -> 150 us (0.974)
  waiting for transfers between devices: 6.06 us -> 2.17 us
    ppermute x4 -> x1, waiting for transfers between devices: 2.99 us -> 0.01 us  [project(): across = lax.ppermute(near, 'c', [(0, 1), (1, 0)])]
  transfers between devices with their start and end apart: 7 -> 4, of which waited for: 4 -> 1; matrix products, arithmetic and copies ran while one was open for 2% -> 2% of each run, Pallas kernels for 2% -> 2%
where the time goes in v3:
time: 150 us
  blocking collectives  114 us (76%)
  Pallas kernels  22 us (15%)
  starting transfers between devices  7.47 us (5%)
  local copies, waits for them, and re-layouts  3.11 us (2%)
  waiting for transfers between devices  2.17 us (1%)
    all_to_all x1, blocking collectives, per_device(): lax.all_to_all(outgoing, AXES, split_axis=0, concat_axis=0, tiled=True)  40.8 us
    all_to_all x1, blocking collectives, per_device(): lax.all_to_all(results, AXES, split_axis=0, concat_axis=0, tiled=True)  39.8 us
    all_to_all x1, blocking collectives, per_device(): lax.all_to_all(partial, ('c', 'y', 'x'), split_axis=0, concat_axis=0, til...  20.2 us
    all_gather x1, blocking collectives, project(): near = lax.all_gather(attended, 'y', axis=0, tiled=True)  13.4 us
    pallas_call x1, Pallas kernels, apply_expert(): pl.pallas_call(expert_kernel, out_shape=jax.ShapeDtypeStruct((count, seg)...  12.2 us
    ppermute x3, starting transfers between devices, project(): lax.ppermute(own, 'z', [(i, (i + k) % zs) for i in range(zs)])  5.29 us
    pallas_call x1, Pallas kernels, project(): return (call(near, across, *pieces), ready)  4.26 us
    pallas_call x1, Pallas kernels, attend(): pl.pallas_call(attend_kernel, out_shape=jax.ShapeDtypeStruct((requests *...  3.31 us
  transfers between devices with their start and end apart: 4, of which 1 were waited for; matrix products, arithmetic and copies ran while one was open for 2% of the time, Pallas kernels for 2%

profile of v3, /device:TPU:1, one launch (start us, length us, event | category | flops | bytes accessed | tf_op | source)
XLA Modules:
  0.0 149.9 jit_solution(858540270755473004)
XLA Ops:
  0.0 0.0 copy-start.6
  0.0 4.6 %collective-permute-start.2 = (bf16[160,1536]{1,0:T(8,128)(2,1)}, bf16[160,1536]{1,0:T(8,128)(2,1)S(1)}, u32[]{:S(2)}, u32[]{:S(2)}) collective-permute-start(bf16[160,1536]{1,0:T(8,128)(2,1)} %bitcast.20), channel_id=1, source_target_pairs={{0,24},{8,0},{16,8},{24,16},{1,25},{9,1},{17,9},{25,17},{2,26},{10... | collective-permute-start | bytes 1474568 | tf_op jit(solution)/shard_map/ppermute | solution.py:146
  4.6 0.0 collective-permute-start.1
  4.6 0.7 collective-permute-start
  5.3 3.3 %attend.1 = bf16[64,1536]{1,0:T(8,128)(2,1)} custom-call(s32[2]{0:T(128)} %counts_hbm.1, s32[2]{0:T(128)} %lengths_hbm.1, bf16[2,32,1536]{2,1,0:T(8,128)(2,1)} %q_hbm.1, bf16[2,512,128]{2,1,0:T(8,128)(2,1)} %k_hbm.1, bf16[2,512,128]{2,1,0:T(8,128)(2,1)} %v_hbm.1, bf16[2,32,128]{2,1,0:T(8,128)(2,1)} %nk_hbm.1, bf16[2,32,128]{2,1,0:T(8,128)(2,1)} %nv_hbm.1), custom_call_target="tpu_custom_call" | custom-call | flops 213909504 | bytes 1048576 | tf_op jit(solution)/shard_map/attend/pallas_call | solution.py:103
  8.6 13.4 %all_gather.3.near_hbm = bf16[256,1536]{1,0:T(8,128)(2,1)S(1)} all-gather(bf16[64,1536]{1,0:T(8,128)(2,1)} %attend.1), channel_id=1, replica_groups=mesh['y'=4,'z'=4,'c'=2,'x'=4] {'y'}, dimensions={0}, use_global_device_ids=true | all-gather | bytes 983040 | tf_op jit(solution)/shard_map/all_gather | solution.py:148
  22.0 0.0 copy-start.2
  22.0 2.2 %collective-permute-start.3 = (bf16[256,1536]{1,0:T(8,128)(2,1)S(1)}, bf16[256,1536]{1,0:T(8,128)(2,1)S(1)}, u32[]{:S(2)}, u32[]{:S(2)}) collective-permute-start(bf16[256,1536]{1,0:T(8,128)(2,1)S(1)} %all_gather.3.near_hbm), channel_id=1, source_target_pairs={{0,4},{4,0},{1,5},{5,1},{2,6},{6,2},{3,7},{7,3},{8,12},{12,8},{9,1... | collective-permute-start | bytes 2359304 | tf_op jit(solution)/shard_map/ppermute | solution.py:149
  24.2 0.8 copy.22
  24.9 0.1 reshape.194
  25.0 0.1 convert_reduce_fusion
  25.2 0.1 select_reduce_fusion.1
  25.3 0.8 copy.23
  26.0 0.1 broadcast_in_dim.88
  26.1 0.1 select_reduce_fusion
  26.3 0.1 broadcast_in_dim.91
  26.4 0.1 reshape.196
  26.5 0.1 broadcast_in_dim.86
  26.6 0.1 reshape.195
  26.8 0.0 copy-done.6
  26.8 0.1 fusion.14
  26.9 0.1 copy.24
  27.0 0.2 fusion.place_ref
  27.2 0.0 copy-start
  27.2 0.0 copy-start.1
  27.2 0.0 collective-permute-done.2.refs_3_
  27.3 0.0 copy-start.4
  27.3 0.0 collective-permute-done.1.refs_2_
  27.3 0.0 copy-start.5
  27.3 2.2 %collective-permute-done.refs_1_ = bf16[160,1536]{1,0:T(8,128)(2,1)} collective-permute-done((bf16[160,1536]{1,0:T(8,128)(2,1)}, bf16[160,1536]{1,0:T(8,128)(2,1)}, u32[]{:S(2)}, u32[]{:S(2)}) %collective-permute-start) | collective-permute-done | bytes 491552 | tf_op jit(solution)/shard_map/ppermute | solution.py:146
  29.5 0.0 collective-permute-done.3.across_hbm
  29.5 0.0 copy-done.2
  29.5 0.0 copy-done.4
  29.5 0.0 copy-done.5
  29.5 0.0 copy-start.3
  29.5 0.9 copy-done.3
  30.4 4.3 %project.1 = bf16[512,640]{1,0:T(8,128)(2,1)} custom-call(bf16[256,1536]{1,0:T(8,128)(2,1)} %copy-done.2, bf16[256,1536]{1,0:T(8,128)(2,1)} %copy-done.3, bf16[160,1536]{1,0:T(8,128)(2,1)} %bitcast.23, bf16[160,1536]{1,0:T(8,128)(2,1)} %collective-permute-done.refs_1_, bf16[160,1536]{1,0:T(8,128)(2,1)} %copy-done.5, bf16[160,1536]{1,0:T(8,128)(2,1)} %copy-done.4), custom_call_target="tpu_custom_call" | custom-call | tf_op jit(solution)/shard_map/project/pallas_call | solution.py:169
  34.6 20.2 %all_to_all.15.arrived_ref = bf16[32,16,640]{2,1,0:T(8,128)(2,1)S(1)} all-to-all(bf16[32,16,640]{2,1,0:T(8,128)(2,1)} %bitcast.19), channel_id=1, replica_groups=mesh['y'=4,'z'=4,'c'=2,'x'=4] {'c','y','x'}, dimensions={0} | all-to-all | bytes 1310720 | tf_op jit(solution)/shard_map/all_to_all | solution.py:388
  54.8 0.0 copy-done
  54.9 0.0 copy-done.1
  54.9 1.1 norm_place.1
  56.0 40.8 %all_to_all.16 = bf16[128,8,1280]{2,1,0:T(8,128)(2,1)S(1)} all-to-all(bf16[128,8,1280]{2,1,0:T(8,128)(2,1)S(1)} %bitcast.14), channel_id=1, replica_groups=mesh['y'=4,'z'=4,'c'=2,'x'=4] {'y','z','c','x'}, dimensions={0} | all-to-all | bytes 5242880 | tf_op jit(solution)/shard_map/all_to_all | solution.py:391
  96.8 12.2 %expert.1 = bf16[1024,1280]{1,0:T(8,128)(2,1)S(1)} custom-call(bf16[1024,1280]{1,0:T(8,128)(2,1)S(1)} %bitcast.11, bf16[5120,768]{1,0:T(8,128)(2,1)} %bitcast.16, bf16[5120,768]{1,0:T(8,128)(2,1)} %bitcast.17, bf16[768,5120]{1,0:T(8,128)(2,1)} %bitcast.18), custom_call_target="tpu_custom_call" | custom-call | tf_op jit(solution)/shard_map/expert/pallas_call | solution.py:282
  109.0 39.8 %all_to_all.17 = bf16[128,8,1280]{2,1,0:T(8,128)(2,1)S(1)} all-to-all(bf16[128,8,1280]{2,1,0:T(8,128)(2,1)S(1)} %bitcast.12), channel_id=1, replica_groups=mesh['y'=4,'z'=4,'c'=2,'x'=4] {'y','z','c','x'}, dimensions={0} | all-to-all | bytes 5242880 | tf_op jit(solution)/shard_map/all_to_all | solution.py:396
  148.7 1.2 combine.1
  (8 shorter events, 0.1 us)
Async XLA Ops:
  0.0 26.8 %copy-start.6 = (s32[2]{0:T(128)S(1)}, s32[2]{0:T(128)}, u32[]{:S(2)}) copy-start(s32[2]{0:T(128)} %counts_hbm.1) | copy-start | bytes 28
  0.0 27.2 %collective-permute-start.2 = (bf16[160,1536]{1,0:T(8,128)(2,1)}, bf16[160,1536]{1,0:T(8,128)(2,1)S(1)}, u32[]{:S(2)}, u32[]{:S(2)}) collective-permute-start(bf16[160,1536]{1,0:T(8,128)(2,1)} %bitcast.20), channel_id=1, source_target_pairs={{0,24},{8,0},{16,8},{24,16},{1,25},{9,1},{17,9},{25,17},{2,26},{10... | collective-permute-start | bytes 1474568 | tf_op jit(solution)/shard_map/ppermute | solution.py:146
  4.6 22.7 %collective-permute-start.1 = (bf16[160,1536]{1,0:T(8,128)(2,1)}, bf16[160,1536]{1,0:T(8,128)(2,1)S(1)}, u32[]{:S(2)}, u32[]{:S(2)}) collective-permute-start(bf16[160,1536]{1,0:T(8,128)(2,1)} %bitcast.21), channel_id=1, source_target_pairs={{0,16},{8,24},{16,0},{24,8},{1,17},{9,25},{17,1},{25,9},{2,18},{10... | collective-permute-start | bytes 1474568 | tf_op jit(solution)/shard_map/ppermute | solution.py:146
  4.6 24.9 %collective-permute-start = (bf16[160,1536]{1,0:T(8,128)(2,1)}, bf16[160,1536]{1,0:T(8,128)(2,1)}, u32[]{:S(2)}, u32[]{:S(2)}) collective-permute-start(bf16[160,1536]{1,0:T(8,128)(2,1)} %bitcast.22), channel_id=1, source_target_pairs={{0,8},{8,16},{16,24},{24,0},{1,9},{9,17},{17,25},{25,1},{2,10},{10... | collective-permute-start | bytes 1474568 | tf_op jit(solution)/shard_map/ppermute | solution.py:146
  22.0 7.4 %copy-start.2 = (bf16[256,1536]{1,0:T(8,128)(2,1)}, bf16[256,1536]{1,0:T(8,128)(2,1)S(1)}, u32[]{:S(2)}) copy-start(bf16[256,1536]{1,0:T(8,128)(2,1)S(1)} %all_gather.3.near_hbm) | copy-start | bytes 2359300
  22.0 7.4 %collective-permute-start.3 = (bf16[256,1536]{1,0:T(8,128)(2,1)S(1)}, bf16[256,1536]{1,0:T(8,128)(2,1)S(1)}, u32[]{:S(2)}, u32[]{:S(2)}) collective-permute-start(bf16[256,1536]{1,0:T(8,128)(2,1)S(1)} %all_gather.3.near_hbm), channel_id=1, source_target_pairs={{0,4},{4,0},{1,5},{5,1},{2,6},{6,2},{3,7},{7,3},{8,12},{12,8},{9,1... | collective-permute-start | bytes 2359304 | tf_op jit(solution)/shard_map/ppermute | solution.py:149
  27.2 27.6 %copy-start = (bf16[16,5120]{1,0:T(8,128)(2,1)S(1)}, bf16[16,5120]{1,0:T(8,128)(2,1)}, u32[]{:S(2)}) copy-start(bf16[16,5120]{1,0:T(8,128)(2,1)} %residual_ref.1) | copy-start | bytes 491524
  27.2 27.6 %copy-start.1 = (f32[5120]{0:T(1024)S(1)}, f32[5120]{0:T(1024)}, u32[]{:S(2)}) copy-start(f32[5120]{0:T(1024)} %param.24) | copy-start | bytes 61444
  27.3 2.2 %copy-start.4 = (bf16[160,1536]{1,0:T(8,128)(2,1)}, bf16[160,1536]{1,0:T(8,128)(2,1)S(1)}, u32[]{:S(2)}) copy-start(bf16[160,1536]{1,0:T(8,128)(2,1)S(1)} %collective-permute-done.2.refs_3_) | copy-start | bytes 1474564
  27.3 2.2 %copy-start.5 = (bf16[160,1536]{1,0:T(8,128)(2,1)}, bf16[160,1536]{1,0:T(8,128)(2,1)S(1)}, u32[]{:S(2)}) copy-start(bf16[160,1536]{1,0:T(8,128)(2,1)S(1)} %collective-permute-done.1.refs_2_) | copy-start | bytes 1474564
  29.5 0.9 copy-start.3

commit v4 on v3

--- a/solution.py
+++ b/solution.py
@@ -70,7 +70,7 @@
     slot = lax.broadcasted_iota(jnp.int32, (rows, slots), 0) % slots
     fresh = lax.broadcasted_iota(jnp.int32, (rows, slots), 1)
     position = lax.broadcasted_iota(jnp.int32, (rows, cached), 1)
-    for copy in copies:
+    for copy in copies[:5]:
         copy.wait()
     for r in range(requests):
         q = jnp.concatenate(
@@ -87,6 +87,9 @@
         new = jnp.exp(new - highest)
         total = jnp.sum(old, axis=1, keepdims=True) + jnp.sum(new, axis=1, keepdims=True)
         inverse = 1.0 / total
+        if r == 0:
+            for copy in copies[5:]:
+                copy.wait()
         mixed = dot((old * inverse).astype(BF), v_ref[r]) + dot(
             (new * inverse).astype(BF), nv_ref[r]
         )
@@ -116,15 +119,12 @@
     )(counts, lengths, *arrays)
 
 
-def project_kernel(homes, near_hbm, across_hbm, *refs):
-    pieces, (out_ref, tokens, weight, sems) = refs[:-4], refs[-4:]
+def project_kernel(homes, near_ref, across_ref, *refs):
+    pieces, (out_ref, weight, sems) = refs[:-3], refs[-3:]
     z, zs, c = lax.axis_index("z"), lax.axis_size("z"), lax.axis_index("c")
     part = pieces[0].shape[0]
-    rows = near_hbm.shape[0]
+    rows = near_ref.shape[0]
     copies = []
-    for i, (block, home) in enumerate(((near_hbm, c), (across_hbm, 1 - c))):
-        at = pl.ds(pl.multiple_of(home * rows, rows), rows)
-        copies.append(pltpu.make_async_copy(block, tokens.at[at, :], sems.at[len(pieces) + i]))
     for i, (piece, back) in enumerate(zip(pieces, homes)):
         home = lax.rem(z + zs - back, zs)
         at = pl.ds(pl.multiple_of(home * part, part), part)
@@ -136,12 +136,14 @@
     columns = out_ref.shape[1]
     for j in range(0, columns, 256):
         at = slice(j, min(j + 256, columns))
-        out_ref[:, at] = dot_t(tokens[...], weight[at, :]).astype(BF)
-
-
-def project(attended, o_weight, route):
+        for block, home in ((near_ref, c), (across_ref, 1 - c)):
+            out_ref[pl.ds(pl.multiple_of(home * rows, rows), rows), at] = dot_t(
+                block[...], weight[at, :]
+            ).astype(BF)
+
+
+def project(attended, own, route):
     zs = lax.axis_size("z")
-    own = o_weight.T
     along = [
         lax.ppermute(own, "z", [(i, (i + k) % zs) for i in range(zs)]) for k in range(1, zs)
     ]
@@ -156,14 +158,13 @@
     call = pl.pallas_call(
         functools.partial(project_kernel, tuple(range(zs))),
         out_shape=jax.ShapeDtypeStruct((rows, columns), BF),
-        in_specs=[pl.BlockSpec(memory_space=pl.ANY)] * (2 + len(pieces)),
+        in_specs=vmem(2) + [pl.BlockSpec(memory_space=pl.ANY)] * len(pieces),
         out_specs=pl.BlockSpec(memory_space=pltpu.VMEM),
         scratch_shapes=[
-            pltpu.VMEM((rows, depth), BF),
             pltpu.VMEM((columns, depth), BF),
-            pltpu.SemaphoreType.DMA((len(pieces) + 2,)),
+            pltpu.SemaphoreType.DMA((len(pieces),)),
         ],
-        compiler_params=pltpu.CompilerParams(vmem_limit_bytes=60 << 20),
+        compiler_params=pltpu.CompilerParams(vmem_limit_bytes=16 << 20),
         name="project",
     )
     return call(near, across, *pieces), ready
@@ -236,9 +237,10 @@
         at = pl.ds(s * seg, seg)
         copies.append(pltpu.make_async_copy(gate_hbm.at[at, :], gate.at[at, :], sems.at[0, s]))
         copies.append(pltpu.make_async_copy(up_hbm.at[at, :], up.at[at, :], sems.at[1, s]))
-    for s in range(SEG):
-        at = pl.ds(s * seg, seg)
-        copies.append(pltpu.make_async_copy(down_hbm.at[:, at], down.at[:, at], sems.at[2, s]))
+    part = down.shape[0] // SEG
+    for s in range(SEG):
+        at = pl.ds(s * part, part)
+        copies.append(pltpu.make_async_copy(down_hbm.at[at, :], down.at[at, :], sems.at[2, s]))
 
     def need(i):
         copies[i].wait()
@@ -267,6 +269,7 @@
     inner[...] = (gate_sum / (1.0 + jnp.exp(-gate_sum)) * up_sum).astype(BF)
     for s in range(SEG):
         need(2 * SEG + s)
+    for s in range(SEG):
         result = dot(inner[...], down[:, pl.ds(s * seg, seg)])
         for k in range(lanes):
             stage[k, pl.ds(s, rows, stride=SEG), :] = result[:, k * LANES : (k + 1) * LANES]
@@ -383,7 +386,7 @@
         ids, weights, _ = lax.optimization_barrier((expert_ids, route_weights, after))
         return (*routing(ids, weights, experts), live)
 
-    partial, (place, shares, live) = project(attended, o_weight, route)
+    partial, (place, shares, live) = project(attended, o_weight.T, route)
     partial = partial.reshape(-1, rows, partial.shape[1])
     arrived = lax.all_to_all(partial, ("c", "y", "x"), split_axis=0, concat_axis=0, tiled=True)
     hidden, outgoing = norm_and_place(arrived, residual, norm_gain[None, :], place)

time: 150 us -> 147 us (0.980)
  Pallas kernels: 22 us -> 19.8 us
where the time goes in v4:
time: 147 us
  blocking collectives  114 us (78%)
  Pallas kernels  19.8 us (13%)
  starting transfers between devices  7.47 us (5%)
  local copies, waits for them, and re-layouts  2.22 us (2%)
  waiting for transfers between devices  2.17 us (1%)
    all_to_all x1, blocking collectives, per_device(): lax.all_to_all(outgoing, AXES, split_axis=0, concat_axis=0, tiled=True)  40.8 us
    all_to_all x1, blocking collectives, per_device(): lax.all_to_all(results, AXES, split_axis=0, concat_axis=0, tiled=True)  39.8 us
    all_to_all x1, blocking collectives, per_device(): lax.all_to_all(partial, ('c', 'y', 'x'), split_axis=0, concat_axis=0, til...  20 us
    all_gather x1, blocking collectives, project(): near = lax.all_gather(attended, 'y', axis=0, tiled=True)  13.4 us
    pallas_call x1, Pallas kernels, apply_expert(): pl.pallas_call(expert_kernel, out_shape=jax.ShapeDtypeStruct((count, seg)...  11.4 us
    ppermute x3, starting transfers between devices, project(): lax.ppermute(own, 'z', [(i, (i + k) % zs) for i in range(zs)])  5.29 us
    pallas_call x1, Pallas kernels, attend(): pl.pallas_call(attend_kernel, out_shape=jax.ShapeDtypeStruct((requests *...  3.33 us
  transfers between devices with their start and end apart: 4, of which 1 were waited for; matrix products, arithmetic and copies ran while one was open for 2% of the time, Pallas kernels for 2%

profile of v4, /device:TPU:1, one launch (start us, length us, event | category | flops | bytes accessed | tf_op | source)
XLA Modules:
  0.0 146.5 jit_solution(537195246524230031)
XLA Ops:
  0.0 0.0 copy-start
  0.0 0.0 copy-start.3
  0.0 4.6 %collective-permute-start.2 = (bf16[160,1536]{1,0:T(8,128)(2,1)}, bf16[160,1536]{1,0:T(8,128)(2,1)S(1)}, u32[]{:S(2)}, u32[]{:S(2)}) collective-permute-start(bf16[160,1536]{1,0:T(8,128)(2,1)} %bitcast.16), channel_id=1, source_target_pairs={{0,24},{8,0},{16,8},{24,16},{1,25},{9,1},{17,9},{25,17},{2,26},{10... | collective-permute-start | bytes 1474568 | tf_op jit(solution)/shard_map/ppermute | solution.py:148
  4.6 0.0 collective-permute-start.1
  4.6 0.7 collective-permute-start
  5.3 3.3 %attend.1 = bf16[64,1536]{1,0:T(8,128)(2,1)} custom-call(s32[2]{0:T(128)} %counts_hbm.1, s32[2]{0:T(128)} %lengths_hbm.1, bf16[2,32,1536]{2,1,0:T(8,128)(2,1)} %q_hbm.1, bf16[2,512,128]{2,1,0:T(8,128)(2,1)} %k_hbm.1, bf16[2,512,128]{2,1,0:T(8,128)(2,1)} %v_hbm.1, bf16[2,32,128]{2,1,0:T(8,128)(2,1)} %nk_hbm.1, bf16[2,32,128]{2,1,0:T(8,128)(2,1)} %nv_hbm.1), custom_call_target="tpu_custom_call" | custom-call | flops 213909504 | bytes 1048576 | tf_op jit(solution)/shard_map/attend/pallas_call | solution.py:106
  8.6 13.4 %all_gather.3.near_ref = bf16[256,1536]{1,0:T(8,128)(2,1)S(1)} all-gather(bf16[64,1536]{1,0:T(8,128)(2,1)} %attend.1), channel_id=1, replica_groups=mesh['y'=4,'z'=4,'c'=2,'x'=4] {'y'}, dimensions={0}, use_global_device_ids=true | all-gather | bytes 983040 | tf_op jit(solution)/shard_map/all_gather | solution.py:150
  22.0 2.2 %collective-permute-start.3 = (bf16[256,1536]{1,0:T(8,128)(2,1)S(1)}, bf16[256,1536]{1,0:T(8,128)(2,1)S(1)}, u32[]{:S(2)}, u32[]{:S(2)}) collective-permute-start(bf16[256,1536]{1,0:T(8,128)(2,1)S(1)} %all_gather.3.near_ref), channel_id=1, source_target_pairs={{0,4},{4,0},{1,5},{5,1},{2,6},{6,2},{3,7},{7,3},{8,12},{12,8},{9,1... | collective-permute-start | bytes 2359304 | tf_op jit(solution)/shard_map/ppermute | solution.py:151
  24.2 0.8 copy.22
  25.0 0.1 reshape.194
  25.1 0.1 convert_reduce_fusion
  25.2 0.1 select_reduce_fusion.1
  25.3 0.8 copy.23
  26.1 0.1 broadcast_in_dim.88
  26.1 0.1 select_reduce_fusion
  26.3 0.1 broadcast_in_dim.91
  26.4 0.1 reshape.196
  26.5 0.1 broadcast_in_dim.86
  26.6 0.1 reshape.195
  26.8 0.0 copy-done.3
  26.8 0.1 fusion.14
  26.9 0.1 copy.24
  27.0 0.2 fusion.place_ref
  27.2 0.0 copy-start.1
  27.3 0.0 copy-start.2
  27.3 0.0 collective-permute-done.2.refs_3_
  27.3 0.0 collective-permute-done.1.refs_2_
  27.3 2.2 %collective-permute-done.refs_1_ = bf16[160,1536]{1,0:T(8,128)(2,1)} collective-permute-done((bf16[160,1536]{1,0:T(8,128)(2,1)}, bf16[160,1536]{1,0:T(8,128)(2,1)}, u32[]{:S(2)}, u32[]{:S(2)}) %collective-permute-start) | collective-permute-done | bytes 491552 | tf_op jit(solution)/shard_map/ppermute | solution.py:148
  29.5 0.0 collective-permute-done.3.across_ref
  29.5 0.0 copy-done
  29.5 2.8 %project.1 = bf16[512,640]{1,0:T(8,128)(2,1)S(1)} custom-call(bf16[256,1536]{1,0:T(8,128)(2,1)S(1)} %all_gather.3.near_ref, bf16[256,1536]{1,0:T(8,128)(2,1)S(1)} %collective-permute-done.3.across_ref, bf16[160,1536]{1,0:T(8,128)(2,1)S(1)} %bitcast.19, bf16[160,1536]{1,0:T(8,128)(2,1)} %collective-permute-done.refs_1_, ...), custom_call_target="tpu_custom_call" | custom-call | tf_op jit(solution)/shard_map/project/pallas_call | solution.py:170
  32.3 20.0 %all_to_all.15.arrived_ref = bf16[32,16,640]{2,1,0:T(8,128)(2,1)S(1)} all-to-all(bf16[32,16,640]{2,1,0:T(8,128)(2,1)S(1)} %bitcast.15), channel_id=1, replica_groups=mesh['y'=4,'z'=4,'c'=2,'x'=4] {'c','y','x'}, dimensions={0} | all-to-all | bytes 1310720 | tf_op jit(solution)/shard_map/all_to_all | solution.py:391
  52.3 0.0 copy-done.1
  52.3 0.0 copy-done.2
  52.3 1.1 norm_place.1
  53.4 40.8 %all_to_all.16 = bf16[128,8,1280]{2,1,0:T(8,128)(2,1)S(1)} all-to-all(bf16[128,8,1280]{2,1,0:T(8,128)(2,1)S(1)} %bitcast.14), channel_id=1, replica_groups=mesh['y'=4,'z'=4,'c'=2,'x'=4] {'y','z','c','x'}, dimensions={0} | all-to-all | bytes 5242880 | tf_op jit(solution)/shard_map/all_to_all | solution.py:394
  94.2 11.4 %expert.1 = bf16[1024,1280]{1,0:T(8,128)(2,1)S(1)} custom-call(bf16[1024,1280]{1,0:T(8,128)(2,1)S(1)} %bitcast.11, bf16[5120,768]{1,0:T(8,128)(2,1)} %bitcast.21, bf16[5120,768]{1,0:T(8,128)(2,1)} %bitcast.22, bf16[768,5120]{1,0:T(8,128)(2,1)} %bitcast.23), custom_call_target="tpu_custom_call" | custom-call | tf_op jit(solution)/shard_map/expert/pallas_call | solution.py:285
  105.6 39.8 %all_to_all.17 = bf16[128,8,1280]{2,1,0:T(8,128)(2,1)S(1)} all-to-all(bf16[128,8,1280]{2,1,0:T(8,128)(2,1)S(1)} %bitcast.12), channel_id=1, replica_groups=mesh['y'=4,'z'=4,'c'=2,'x'=4] {'y','z','c','x'}, dimensions={0} | all-to-all | bytes 5242880 | tf_op jit(solution)/shard_map/all_to_all | solution.py:399
  145.4 1.2 combine.1
  (8 shorter events, 0.1 us)
Async XLA Ops:
  0.0 29.5 %copy-start = (bf16[1536,160]{0,1:T(8,128)(2,1)S(1)}, bf16[1536,160]{0,1:T(8,128)(2,1)}, u32[]{:S(2)}) copy-start(bf16[1536,160]{0,1:T(8,128)(2,1)} %param.23) | copy-start | bytes 1474564
  0.0 26.8 %copy-start.3 = (s32[2]{0:T(128)S(1)}, s32[2]{0:T(128)}, u32[]{:S(2)}) copy-start(s32[2]{0:T(128)} %counts_hbm.1) | copy-start | bytes 28
  0.0 27.3 %collective-permute-start.2 = (bf16[160,1536]{1,0:T(8,128)(2,1)}, bf16[160,1536]{1,0:T(8,128)(2,1)S(1)}, u32[]{:S(2)}, u32[]{:S(2)}) collective-permute-start(bf16[160,1536]{1,0:T(8,128)(2,1)} %bitcast.16), channel_id=1, source_target_pairs={{0,24},{8,0},{16,8},{24,16},{1,25},{9,1},{17,9},{25,17},{2,26},{10... | collective-permute-start | bytes 1474568 | tf_op jit(solution)/shard_map/ppermute | solution.py:148
  4.6 22.7 %collective-permute-start.1 = (bf16[160,1536]{1,0:T(8,128)(2,1)}, bf16[160,1536]{1,0:T(8,128)(2,1)S(1)}, u32[]{:S(2)}, u32[]{:S(2)}) collective-permute-start(bf16[160,1536]{1,0:T(8,128)(2,1)} %bitcast.17), channel_id=1, source_target_pairs={{0,16},{8,24},{16,0},{24,8},{1,17},{9,25},{17,1},{25,9},{2,18},{10... | collective-permute-start | bytes 1474568 | tf_op jit(solution)/shard_map/ppermute | solution.py:148
  4.6 24.9 %collective-permute-start = (bf16[160,1536]{1,0:T(8,128)(2,1)}, bf16[160,1536]{1,0:T(8,128)(2,1)}, u32[]{:S(2)}, u32[]{:S(2)}) collective-permute-start(bf16[160,1536]{1,0:T(8,128)(2,1)} %bitcast.18), channel_id=1, source_target_pairs={{0,8},{8,16},{16,24},{24,0},{1,9},{9,17},{17,25},{25,1},{2,10},{10... | collective-permute-start | bytes 1474568 | tf_op jit(solution)/shard_map/ppermute | solution.py:148
  22.0 7.4 %collective-permute-start.3 = (bf16[256,1536]{1,0:T(8,128)(2,1)S(1)}, bf16[256,1536]{1,0:T(8,128)(2,1)S(1)}, u32[]{:S(2)}, u32[]{:S(2)}) collective-permute-start(bf16[256,1536]{1,0:T(8,128)(2,1)S(1)} %all_gather.3.near_ref), channel_id=1, source_target_pairs={{0,4},{4,0},{1,5},{5,1},{2,6},{6,2},{3,7},{7,3},{8,12},{12,8},{9,1... | collective-permute-start | bytes 2359304 | tf_op jit(solution)/shard_map/ppermute | solution.py:151
  27.2 25.0 %copy-start.1 = (bf16[16,5120]{1,0:T(8,128)(2,1)S(1)}, bf16[16,5120]{1,0:T(8,128)(2,1)}, u32[]{:S(2)}) copy-start(bf16[16,5120]{1,0:T(8,128)(2,1)} %residual_ref.1) | copy-start | bytes 491524
  27.3 25.0 %copy-start.2 = (f32[5120]{0:T(1024)S(1)}, f32[5120]{0:T(1024)}, u32[]{:S(2)}) copy-start(f32[5120]{0:T(1024)} %param.24) | copy-start | bytes 61444

commit v5 on v4

--- a/solution.py
+++ b/solution.py
@@ -145,7 +145,7 @@
 def project(attended, own, route):
     zs = lax.axis_size("z")
     along = [
-        lax.ppermute(own, "z", [(i, (i + k) % zs) for i in range(zs)]) for k in range(1, zs)
+        lax.ppermute(own, "z", [(i, (i + k) % zs) for i in range(zs)]) for k in (1, 3, 2)
     ]
     near = lax.all_gather(attended, "y", axis=0, tiled=True)
     across = lax.ppermute(near, "c", [(0, 1), (1, 0)])
@@ -156,7 +156,7 @@
     part, depth = own.shape
     columns = part * zs
     call = pl.pallas_call(
-        functools.partial(project_kernel, tuple(range(zs))),
+        functools.partial(project_kernel, (0, 1, 3, 2)),
         out_shape=jax.ShapeDtypeStruct((rows, columns), BF),
         in_specs=vmem(2) + [pl.BlockSpec(memory_space=pl.ANY)] * len(pieces),
         out_specs=pl.BlockSpec(memory_space=pltpu.VMEM),

time: 147 us -> 146 us (level)
  waiting for transfers between devices: 2.17 us -> 0.01 us
    ppermute x3, waiting for transfers between devices: 2.17 us -> 0.01 us  [project(): lax.ppermute(own, 'z', [(i, (i + k) % zs) for i in range(zs)])]
  transfers between devices with their start and end apart: 4 -> 4, of which waited for: 1 -> 0; matrix products, arithmetic and copies ran while one was open for 2% -> 2% of each run, Pallas kernels for 2% -> 2%
where the time goes in v5:
time: 146 us
  blocking collectives  115 us (79%)
  Pallas kernels  19.8 us (14%)
  starting transfers between devices  7.97 us (5%)
  local copies, waits for them, and re-layouts  2.22 us (2%)
    all_to_all x1, blocking collectives, per_device(): lax.all_to_all(outgoing, AXES, split_axis=0, concat_axis=0, tiled=True)  42 us
    all_to_all x1, blocking collectives, per_device(): lax.all_to_all(results, AXES, split_axis=0, concat_axis=0, tiled=True)  39.8 us
    all_to_all x1, blocking collectives, per_device(): lax.all_to_all(partial, ('c', 'y', 'x'), split_axis=0, concat_axis=0, til...  19.6 us
    all_gather x1, blocking collectives, project(): near = lax.all_gather(attended, 'y', axis=0, tiled=True)  13.5 us
    pallas_call x1, Pallas kernels, apply_expert(): pl.pallas_call(expert_kernel, out_shape=jax.ShapeDtypeStruct((count, seg)...  11.4 us
    ppermute x3, starting transfers between devices, project(): lax.ppermute(own, 'z', [(i, (i + k) % zs) for i in range(zs)])  5.89 us
    pallas_call x1, Pallas kernels, attend(): pl.pallas_call(attend_kernel, out_shape=jax.ShapeDtypeStruct((requests *...  3.33 us
  transfers between devices with their start and end apart: 4, of which 0 were waited for; matrix products, arithmetic and copies ran while one was open for 2% of the time, Pallas kernels for 2%

profile of v5, /device:TPU:1, one launch (start us, length us, event | category | flops | bytes accessed | tf_op | source)
XLA Modules:
  0.0 145.9 jit_solution(8124922886105431790)
XLA Ops:
  0.0 0.0 copy-start
  0.0 0.0 copy-start.3
  0.0 4.4 %collective-permute-start.2 = (bf16[160,1536]{1,0:T(8,128)(2,1)}, bf16[160,1536]{1,0:T(8,128)(2,1)S(1)}, u32[]{:S(2)}, u32[]{:S(2)}) collective-permute-start(bf16[160,1536]{1,0:T(8,128)(2,1)} %bitcast.16), channel_id=1, source_target_pairs={{0,16},{8,24},{16,0},{24,8},{1,17},{9,25},{17,1},{25,9},{2,18},{10... | collective-permute-start | bytes 1474568 | tf_op jit(solution)/shard_map/ppermute | solution.py:148
  4.4 0.4 collective-permute-start.1
  4.9 1.0 collective-permute-start
  5.9 3.3 %attend.1 = bf16[64,1536]{1,0:T(8,128)(2,1)} custom-call(s32[2]{0:T(128)} %counts_hbm.1, s32[2]{0:T(128)} %lengths_hbm.1, bf16[2,32,1536]{2,1,0:T(8,128)(2,1)} %q_hbm.1, bf16[2,512,128]{2,1,0:T(8,128)(2,1)} %k_hbm.1, bf16[2,512,128]{2,1,0:T(8,128)(2,1)} %v_hbm.1, bf16[2,32,128]{2,1,0:T(8,128)(2,1)} %nk_hbm.1, bf16[2,32,128]{2,1,0:T(8,128)(2,1)} %nv_hbm.1), custom_call_target="tpu_custom_call" | custom-call | flops 213909504 | bytes 1048576 | tf_op jit(solution)/shard_map/attend/pallas_call | solution.py:106
  9.2 13.5 %all_gather.3.near_ref = bf16[256,1536]{1,0:T(8,128)(2,1)S(1)} all-gather(bf16[64,1536]{1,0:T(8,128)(2,1)} %attend.1), channel_id=1, replica_groups=mesh['y'=4,'z'=4,'c'=2,'x'=4] {'y'}, dimensions={0}, use_global_device_ids=true | all-gather | bytes 983040 | tf_op jit(solution)/shard_map/all_gather | solution.py:150
  22.7 2.1 %collective-permute-start.3 = (bf16[256,1536]{1,0:T(8,128)(2,1)S(1)}, bf16[256,1536]{1,0:T(8,128)(2,1)S(1)}, u32[]{:S(2)}, u32[]{:S(2)}) collective-permute-start(bf16[256,1536]{1,0:T(8,128)(2,1)S(1)} %all_gather.3.near_ref), channel_id=1, source_target_pairs={{0,4},{4,0},{1,5},{5,1},{2,6},{6,2},{3,7},{7,3},{8,12},{12,8},{9,1... | collective-permute-start | bytes 2359304 | tf_op jit(solution)/shard_map/ppermute | solution.py:151
  24.8 0.8 copy.22
  25.6 0.1 reshape.194
  25.7 0.1 convert_reduce_fusion
  25.8 0.1 select_reduce_fusion.1
  25.9 0.8 copy.23
  26.7 0.1 broadcast_in_dim.88
  26.7 0.1 select_reduce_fusion
  26.9 0.1 broadcast_in_dim.91
  27.0 0.1 reshape.196
  27.1 0.1 broadcast_in_dim.86
  27.2 0.1 reshape.195
  27.4 0.0 copy-done.3
  27.4 0.1 fusion.14
  27.5 0.1 copy.24
  27.6 0.2 fusion.place_ref
  27.8 0.0 copy-start.1
  27.9 0.0 copy-start.2
  27.9 0.0 collective-permute-done.2.refs_3_
  27.9 0.0 collective-permute-done.1.refs_2_
  27.9 0.0 collective-permute-done.refs_1_
  27.9 0.0 collective-permute-done.3.across_ref
  27.9 0.0 copy-done
  27.9 2.8 %project.1 = bf16[512,640]{1,0:T(8,128)(2,1)S(1)} custom-call(bf16[256,1536]{1,0:T(8,128)(2,1)S(1)} %all_gather.3.near_ref, bf16[256,1536]{1,0:T(8,128)(2,1)S(1)} %collective-permute-done.3.across_ref, bf16[160,1536]{1,0:T(8,128)(2,1)S(1)} %bitcast.19, bf16[160,1536]{1,0:T(8,128)(2,1)} %collective-permute-done.refs_1_, ...), custom_call_target="tpu_custom_call" | custom-call | tf_op jit(solution)/shard_map/project/pallas_call | solution.py:170
  30.7 19.6 %all_to_all.15.arrived_ref = bf16[32,16,640]{2,1,0:T(8,128)(2,1)S(1)} all-to-all(bf16[32,16,640]{2,1,0:T(8,128)(2,1)S(1)} %bitcast.15), channel_id=1, replica_groups=mesh['y'=4,'z'=4,'c'=2,'x'=4] {'c','y','x'}, dimensions={0} | all-to-all | bytes 1310720 | tf_op jit(solution)/shard_map/all_to_all | solution.py:391
  50.4 0.0 copy-done.1
  50.4 0.0 copy-done.2
  50.4 1.1 norm_place.1
  51.5 42.0 %all_to_all.16 = bf16[128,8,1280]{2,1,0:T(8,128)(2,1)S(1)} all-to-all(bf16[128,8,1280]{2,1,0:T(8,128)(2,1)S(1)} %bitcast.14), channel_id=1, replica_groups=mesh['y'=4,'z'=4,'c'=2,'x'=4] {'y','z','c','x'}, dimensions={0} | all-to-all | bytes 5242880 | tf_op jit(solution)/shard_map/all_to_all | solution.py:394
  93.5 11.4 %expert.1 = bf16[1024,1280]{1,0:T(8,128)(2,1)S(1)} custom-call(bf16[1024,1280]{1,0:T(8,128)(2,1)S(1)} %bitcast.11, bf16[5120,768]{1,0:T(8,128)(2,1)} %bitcast.21, bf16[5120,768]{1,0:T(8,128)(2,1)} %bitcast.22, bf16[768,5120]{1,0:T(8,128)(2,1)} %bitcast.23), custom_call_target="tpu_custom_call" | custom-call | tf_op jit(solution)/shard_map/expert/pallas_call | solution.py:285
  104.9 39.8 %all_to_all.17 = bf16[128,8,1280]{2,1,0:T(8,128)(2,1)S(1)} all-to-all(bf16[128,8,1280]{2,1,0:T(8,128)(2,1)S(1)} %bitcast.12), channel_id=1, replica_groups=mesh['y'=4,'z'=4,'c'=2,'x'=4] {'y','z','c','x'}, dimensions={0} | all-to-all | bytes 5242880 | tf_op jit(solution)/shard_map/all_to_all | solution.py:399
  144.7 1.2 combine.1
  (8 shorter events, 0.1 us)
Async XLA Ops:
  0.0 27.9 %copy-start = (bf16[1536,160]{0,1:T(8,128)(2,1)S(1)}, bf16[1536,160]{0,1:T(8,128)(2,1)}, u32[]{:S(2)}) copy-start(bf16[1536,160]{0,1:T(8,128)(2,1)} %param.23) | copy-start | bytes 1474564
  0.0 27.4 %copy-start.3 = (s32[2]{0:T(128)S(1)}, s32[2]{0:T(128)}, u32[]{:S(2)}) copy-start(s32[2]{0:T(128)} %counts_hbm.1) | copy-start | bytes 28
  0.0 27.9 %collective-permute-start.2 = (bf16[160,1536]{1,0:T(8,128)(2,1)}, bf16[160,1536]{1,0:T(8,128)(2,1)S(1)}, u32[]{:S(2)}, u32[]{:S(2)}) collective-permute-start(bf16[160,1536]{1,0:T(8,128)(2,1)} %bitcast.16), channel_id=1, source_target_pairs={{0,16},{8,24},{16,0},{24,8},{1,17},{9,25},{17,1},{25,9},{2,18},{10... | collective-permute-start | bytes 1474568 | tf_op jit(solution)/shard_map/ppermute | solution.py:148
  4.4 23.4 %collective-permute-start.1 = (bf16[160,1536]{1,0:T(8,128)(2,1)}, bf16[160,1536]{1,0:T(8,128)(2,1)S(1)}, u32[]{:S(2)}, u32[]{:S(2)}) collective-permute-start(bf16[160,1536]{1,0:T(8,128)(2,1)} %bitcast.17), channel_id=1, source_target_pairs={{0,24},{8,0},{16,8},{24,16},{1,25},{9,1},{17,9},{25,17},{2,26},{10... | collective-permute-start | bytes 1474568 | tf_op jit(solution)/shard_map/ppermute | solution.py:148
  4.9 23.0 %collective-permute-start = (bf16[160,1536]{1,0:T(8,128)(2,1)}, bf16[160,1536]{1,0:T(8,128)(2,1)}, u32[]{:S(2)}, u32[]{:S(2)}) collective-permute-start(bf16[160,1536]{1,0:T(8,128)(2,1)} %bitcast.18), channel_id=1, source_target_pairs={{0,8},{8,16},{16,24},{24,0},{1,9},{9,17},{17,25},{25,1},{2,10},{10... | collective-permute-start | bytes 1474568 | tf_op jit(solution)/shard_map/ppermute | solution.py:148
  22.7 5.2 %collective-permute-start.3 = (bf16[256,1536]{1,0:T(8,128)(2,1)S(1)}, bf16[256,1536]{1,0:T(8,128)(2,1)S(1)}, u32[]{:S(2)}, u32[]{:S(2)}) collective-permute-start(bf16[256,1536]{1,0:T(8,128)(2,1)S(1)} %all_gather.3.near_ref), channel_id=1, source_target_pairs={{0,4},{4,0},{1,5},{5,1},{2,6},{6,2},{3,7},{7,3},{8,12},{12,8},{9,1... | collective-permute-start | bytes 2359304 | tf_op jit(solution)/shard_map/ppermute | solution.py:151
  27.8 22.5 %copy-start.1 = (bf16[16,5120]{1,0:T(8,128)(2,1)S(1)}, bf16[16,5120]{1,0:T(8,128)(2,1)}, u32[]{:S(2)}) copy-start(bf16[16,5120]{1,0:T(8,128)(2,1)} %residual_ref.1) | copy-start | bytes 491524
  27.9 22.5 %copy-start.2 = (f32[5120]{0:T(1024)S(1)}, f32[5120]{0:T(1024)}, u32[]{:S(2)}) copy-start(f32[5120]{0:T(1024)} %param.24) | copy-start | bytes 61444
